TPU v7x, 32 devices: a whole 2x2x4 slice. The times are simulated.
32 devices in a mesh: grp: 2 (over x), sub: 16 (over z, y, core).
Axes of the slice: x: 2, y: 2, z: 4, core: 2. Of those that a mesh axis runs over, the one named last changes fastest.
Arguments:
- overall_quantity_unnormalized: float32 [16, 16, 256, 128], P(None, 'grp', 'sub'), may hold values from 0.05 to 1
- reservoir_pressure_field: float32 [16, 256, 128], P('grp', 'sub'), may hold values from 0.7 to 1.3
- reservoir_heat_level: float32 [16, 256, 128], P('grp', 'sub'), may hold values from 0.9 to 1.2
- condensed_flag: int32 [16, 256, 128], P('grp', 'sub'), may hold values 0 or 1
- permeability_field: float32 [16, 256, 128], P('grp', 'sub'), may hold values from 0.1 to 10
- pore_capacity: float32 [16, 256, 128], P('grp', 'sub'), may hold values from 0.05 to 0.3
- former_chemical_quantity: float32 [16, 16, 256, 128], P(None, 'grp', 'sub'), may hold values from 0 to 0.03
- transmissibility_multipliers: float32 [3], replicated, may hold values from 0.3 to 3
- viscosity_pair: float32 [2], replicated, may hold values from 0.3 to 3
- crit_kelvin_values: float32 [16], replicated, may hold values from 0.3 to 2.5
- attraction_parameters: float32 [16], replicated, may hold values from 0.3 to 4
- repulsive_parameters: float32 [16], replicated, may hold values from 0.02 to 0.15
- attraction_thermal_gradients: float32 [16], replicated, may hold values from 0.3 to 1.2
- binary_coupling_matrix: float32 [16, 16], replicated, may hold values from 0 to 0.3, as said below
- injected_recipe_unnormalized: float32 [16], replicated, may hold values from 0.05 to 1
- perforated_locale: int32 [8192], P(('grp', 'sub')), may hold values from 0 to 16383
- perforated_member: int32 [8192, 1], P(('grp', 'sub')), may hold values from 0 to 15; in each aligned block of 256 rows (0 to 255, 256 to 511, ...) at most 40 rows name the same one
- connection_conduit_piece: int32 [8192], P(('grp', 'sub')), may hold values from 0 to 31
- connection_inflow_strength: float32 [8192], P(('grp', 'sub')), may hold values from 0.02 to 0.2
- group_member_place: int32 [2, 16], P('grp'), may hold values from 0 to 15, each once within a row
- conduit_pieces_toe_forward: int32 [32, 32], P(('grp', 'sub')), may hold values from 0 to 31, each once within a row
- conduit_piece_pressures: float32 [32, 32], P(('grp', 'sub')), may hold values from 0.7 to 1.3
- downstream_exit_pressure: float32 [32], P(('grp', 'sub')), may hold values from 0.6 to 1.2
- friction_factors: float32 [32], P(('grp', 'sub')), may hold values from 3.0517578e-05 to 0.00030517578
Outputs:
- residual: float32 [16, 16, 256, 128], P(None, 'grp', 'sub')
- ln_phi: bfloat16 [16, 16, 256, 128], P(None, 'grp', 'sub')
- well_residual: float32 [32, 32], P(('grp', 'sub'))
Inputs may be any that keep to these rules, and one draw needn't show every extreme that they name: `perforated_locale`: flattened index (first, second, layer) of a cell of the listing device's own block. `perforated_member`: a well of the listing device's group; among the 256 rows of one device at most 40 name the same well. `group_member_place`: each row is a permutation; slot j of a group lies on the group's device j. `conduit_pieces_toe_forward`: each row is a permutation of the segments. `binary_coupling_matrix`: symmetric with zero diagonal.
All inputs are finite; a program needn't handle non-finite values. No bound on the sum of `condensed_flag` on one device may be relied on, other than what follows from the above.
Results may differ from a plain program's by a relative error of at most 0.001.
Values sent between devices are 32-bit elements; how exact they have to be, the bound alone decides.
No kernel may reach another device: no remote copies, remote signals or barrier semaphores. Data moves between devices by JAX's collectives and lax.ppermute only.
A program may use at most 64 MiB of HBM per device.

v0:
```python
import functools
import math

import jax
import jax.numpy as jnp
from jax import lax
from jax.experimental import pallas as pl
from jax.experimental.pallas import tpu as pltpu
from jax.sharding import PartitionSpec as P

NEWT = 8
ROOT_TWO = math.sqrt(2.0)
LANES = 128
SUBLANES = 8
F32 = jnp.float32
BF16 = jnp.bfloat16
VMEM_LIMIT = 48 * 1024 * 1024
MARGIN = 8
WHOLE = (
    "coupling", "crit", "attract", "slope", "covol", "heat", "press", "loc", "member", "place",
    "flag", "visc", "trans", "inject", "seg", "strength", "own_press", "perm",
)


def iota(shape, dim):
    return lax.broadcasted_iota(jnp.int32, shape, dim)


def pieces_of(x, count):
    out = []
    for _ in range(count):
        piece = x.astype(BF16)
        out.append(piece)
        x = x - piece.astype(F32)
    return out


def mat(a, b):
    return lax.dot_general(a, b, (((1,), (0,)), ((), ())), preferred_element_type=F32)


def mat_nt(a, b):
    return lax.dot_general(a, b, (((1,), (1,)), ((), ())), preferred_element_type=F32)


def mat_hot(x, hot, count=3):
    return sum(mat(piece, hot) for piece in pieces_of(x, count))


def hot_mat_nt(hot, x, count=3):
    return sum(mat_nt(hot, piece) for piece in pieces_of(x, count))


def inverse(x):
    r = pl.reciprocal(x, approx=True)
    return r * (2.0 - x * r)


def hot(cond):
    return jnp.where(cond, 1.0, 0.0).astype(BF16)


def place_hots(loc, rows):
    n = loc.shape[1]
    row_hot = iota((rows, n), 0) == loc // LANES
    lane_hot = iota((LANES, n), 0) == loc % LANES
    return row_hot, lane_hot


def slot_hot_of(member, place, own):
    wells = place.shape[1]
    half = wells // 2
    row = iota((wells, wells), 0)
    parity = jnp.where(row < half, own % 2, 1 - own % 2)
    slot_of = hot(wells - 2 - 2 * (row % half) + parity == place)
    member_hot = hot(iota((wells, member.shape[1]), 0) == member)
    return mat(slot_of, member_hot)


def phase_kernel(
    nx,
    ny,
    axes,
    amount,
    *rest,
):
    sources, rest = rest[: len(WHOLE)], rest[len(WHOLE) :]
    (
        lnphi_out,
        carried_out,
        mob_out,
        edge_x_out,
        edge_ya_out,
        edge_yb_out,
        part_out,
        pcell_out,
        consts_out,
    ) = rest[:9]
    targets, rest = rest[9 : 9 + len(WHOLE)], rest[9 + len(WHOLE) :]
    amount_v, split_v, psi_v, lnphi_v, field_v, terms_v, table_v, small_sems, in_sems, out_sems = rest
    nc = amount.shape[0]
    per = 2
    chunks = nx // per
    half = chunks // 2
    rows = per * ny

    def go(source, target, sem):
        copy = pltpu.make_async_copy(source, target, sem)
        copy.start()
        return copy

    loads, copies = [], {}
    for k, name in enumerate(WHOLE):
        if name in ("press", "flag"):
            span = pl.ds(len(loads) * half * rows, half * rows)
            loads.append(go(amount.at[:, span], amount_v.at[:, span], in_sems.at[len(loads)]))
        copies[name] = go(sources[k], targets[k], small_sems.at[k])

    def arrived(*names):
        return [targets[WHOLE.index(name)] for name in names]

    for copy in [*copies.values(), *loads]:
        copy.wait()

    size = nc * ny
    spread = hot(iota((size, nc), 0) // ny == iota((size, nc), 1))
    same_row = iota((size, size), 0) % ny == iota((size, size), 1) % ny
    mixers = []
    (coupling,) = arrived("coupling")
    for piece in pieces_of(1.0 - coupling[...], 2):
        wide = mat(spread, piece).astype(BF16)
        mixers.append(jnp.where(same_row, mat_nt(wide, spread), 0.0).astype(BF16))
    mixer = jnp.concatenate([mixers[0], mixers[0], mixers[1]], axis=1)

    crit, attract, slope, covol = arrived("crit", "attract", "slope", "covol")
    for i in range(nc):
        root = jnp.sqrt(jnp.full((SUBLANES, LANES), attract[i], F32))
        kappa = jnp.full((SUBLANES, LANES), slope[i], F32)
        tc = jnp.full((SUBLANES, LANES), crit[i], F32)
        table_v[0, i] = root * (1.0 + kappa)
        table_v[1, i] = root * kappa / jnp.sqrt(tc)
        table_v[2, i] = jnp.full((SUBLANES, LANES), covol[i], F32)

    press, loc, member, place = arrived("press", "loc", "member", "place")
    row_hot, lane_hot = place_hots(loc[...], nx * ny)
    lane_hot = hot(lane_hot)

    def cells_of(field, count):
        found = mat_hot(field, lane_hot, count)
        return jnp.sum(jnp.where(row_hot, found, 0.0), axis=0, keepdims=True)

    p_cell = cells_of(press[...], 3)
    pcell_out[...] = p_cell
    own_slot = lax.axis_index(axes[1])
    slot_hot = slot_hot_of(member[...], place[...], own_slot).astype(BF16)
    (heat,) = arrived("heat")

    shape3 = (ny // SUBLANES, SUBLANES, LANES)
    root_t = [jnp.sqrt(heat[pl.ds(x * ny, ny)].reshape(shape3)) for x in range(nx)]
    for x in range(nx):
        span, lanes = pl.ds(x * ny, ny), pl.ds(x * LANES, LANES)
        total = jnp.zeros(shape3, F32)
        volume = jnp.zeros(shape3, F32)
        for i in range(nc):
            o = amount_v[i, span].reshape(shape3)
            v = jnp.abs(table_v[0, i] - table_v[1, i] * root_t[x]) * o
            total += o
            volume += table_v[2, i] * o
            high, low = pieces_of(v.reshape(ny, LANES), 2)
            split_v[pl.ds(i * ny, ny), lanes] = high
            split_v[pl.ds(size + i * ny, ny), lanes] = low
            split_v[pl.ds(2 * size + i * ny, ny), lanes] = high
        field_v[0, span] = total.reshape(ny, LANES)
        field_v[1, span] = volume.reshape(ny, LANES)
    for c in range(chunks):
        mixed = mat(mixer, split_v[:, pl.ds(c * per * LANES, per * LANES)])
        for k in range(per):
            x = c * per + k
            span = pl.ds(x * ny, ny)
            total = jnp.zeros(shape3, F32)
            for i in range(nc):
                m = mixed[i * ny : (i + 1) * ny, k * LANES : (k + 1) * LANES].reshape(shape3)
                psi = jnp.abs(table_v[0, i] - table_v[1, i] * root_t[x]) * m
                total += amount_v[i, span].reshape(shape3) * psi
                psi_v[i, span] = psi.reshape(ny, LANES)
            field_v[2, span] = total.reshape(ny, LANES)

    flag, visc, trans, inject = arrived("flag", "visc", "trans", "inject")
    states = []
    for h in range(2):
        span = pl.ds(h * half * rows, half * rows)
        p, t = press[span], heat[span]
        liquid = flag[span] == 1
        r = inverse(field_v[0, span])
        rt = inverse(t)
        ratio_pt = p * rt
        beta = field_v[1, span] * r
        gr = ratio_pt * rt * r
        big_a = gr * r * field_v[2, span]
        big_b = ratio_pt * beta
        z = jnp.where(liquid, big_b + 0.01, 1.0 + big_b)
        c1 = big_a - 3.0 * big_b * big_b - 2.0 * big_b
        c0 = big_b * big_b + big_b * big_b * big_b - big_a * big_b
        states.append([z, big_b, big_b + 0.01, big_b - 1.0, c1, c0])
        field_v[1, span] = inverse(beta)
        field_v[3, span] = r
        terms_v[0, span] = ratio_pt
        terms_v[1, span] = 0.5 * big_a
        terms_v[2, span] = gr
    for _ in range(NEWT):
        for state in states:
            z, _, floor, c2, c1, c0 = state
            near = z + c2
            value = (near * z + c1) * z + c0
            incline = (near + near + z) * z + c1
            state[0] = jnp.maximum(z - value * inverse(jnp.maximum(incline, 0.1)), floor)
    for h, (z, big_b, *_) in enumerate(states):
        span = pl.ds(h * half * rows, half * rows)
        ratio_pt, gr = terms_v[0, span], terms_v[2, span]
        log_ratio = jnp.log(
            (z + (1.0 + ROOT_TWO) * big_b) * inverse(z + (1.0 - ROOT_TWO) * big_b)
        )
        lb = log_ratio * inverse(ROOT_TWO * big_b)
        mob = ratio_pt * inverse(z * jnp.where(flag[span] == 1, visc[1], visc[0]))
        mob_out[span] = mob
        field_v[3, span] = mob * field_v[3, span]
        terms_v[0, span] = jnp.log(z - big_b)
        terms_v[1, span] = (z - 1.0 + terms_v[1, span] * lb) * field_v[1, span]
        terms_v[2, span] = gr * lb
    stores = []
    for x in range(nx):
        span = pl.ds(x * ny, ny)
        e0, e1, e2, mr = (
            a.reshape(shape3)
            for a in (terms_v[0, span], terms_v[1, span], terms_v[2, span], field_v[3, span])
        )
        for i in range(nc):
            value = table_v[2, i] * e1 - e0 - psi_v[i, span].reshape(shape3) * e2
            lnphi_v[i, span] = value.reshape(ny, LANES).astype(BF16)
            carried = (mr * amount_v[i, span].reshape(shape3)).reshape(ny, LANES)
            carried_out[i, pl.ds(MARGIN + x * ny, ny)] = carried
        if (x + 1) * 2 % nx == 0:
            span = pl.ds((x + 1 - nx // 2) * ny, nx // 2 * ny)
            stores.append(go(lnphi_v.at[:, span], lnphi_out.at[:, span], out_sems.at[len(stores)]))

    total = sum(inject[i] for i in range(nc))
    share = 1.0 / jnp.full((SUBLANES, LANES), total, F32)
    numbers = [trans[0], trans[1], trans[2], visc[0], visc[1]]
    for i in range(nc):
        consts_out[i] = inject[i] * share
    for i, number in enumerate(numbers):
        consts_out[nc + i] = jnp.full((SUBLANES, LANES), number, F32)

    seg, strength, own_press, perm = arrived("seg", "strength", "own_press", "perm")
    weight = strength[...] * cells_of(mob_out[...], 2)
    segments = own_press.shape[1]
    place_of = iota((LANES, loc.shape[1]), 0)
    sums = jnp.where(place_of == seg[...], weight, 0.0)
    sums += jnp.where(place_of == seg[...] + segments, weight * (p_cell - 1.0), 0.0)
    sums = hot_mat_nt(slot_hot, sums, 2)
    half = sums.shape[0] // 2
    for k in range(2):
        shift = hot(iota((segments, LANES), 0) + (2 + k) * segments == iota((segments, LANES), 1))
        with_press = sums[k * half : (k + 1) * half] + mat_hot(own_press[...], shift)
        if k == 0:
            part_out[...] = with_press
        else:
            edge_ya_out[pl.ds(nc + 2, half // nx)] = with_press.reshape(half // nx, nx, LANES)

    odd_g = lax.axis_index(axes[0]) % 2 == 1
    odd_s = own_slot % 2 == 1
    for k in range(edge_x_out.shape[0]):
        at_low = odd_g if k == 0 else jnp.logical_not(odd_g)
        start = pl.multiple_of(jnp.where(at_low, 0, (nx - 1) * ny), ny)
        for i in range(nc):
            edge_x_out[k, i] = carried_out[i, pl.ds(start + MARGIN, ny)]
        edge_x_out[k, nc] = press[pl.ds(start, ny)]
        edge_x_out[k, nc + 1] = perm[pl.ds(start, ny)]
    for i in range(nc + 2):
        source = carried_out.at[i] if i < nc else press if i == nc else perm
        skip = MARGIN if i < nc else 0
        low = source[pl.ds(skip, nx, stride=ny)]
        high = source[pl.ds(skip + ny - 1, nx, stride=ny)]
        edge_ya_out[i] = jnp.where(odd_s, low, high)
        edge_yb_out[i] = jnp.where(odd_s, high, low)
    for copy in stores:
        copy.wait()


def flux_kernel(
    nx,
    ny,
    axes,
    many_x,
    carried,
    press,
    perm,
    pore,
    flag,
    old,
    mob,
    edge_ya,
    edge_yb,
    well_rows,
    loc,
    member,
    seg,
    strength,
    place,
    pcell,
    consts,
    own_press,
    order,
    exit_press,
    friction,
    *rest,
):
    edge_x, rest = rest[:many_x], rest[many_x:]
    resid_out, well_out, y_v, res_v, out_sems = rest
    nc = carried.shape[0]
    g, s = lax.axis_index(axes[0]), lax.axis_index(axes[1])
    ng, ns = lax.axis_size(axes[0]), lax.axis_size(axes[1])
    odd_g, odd_s = g % 2 == 1, s % 2 == 1
    has_low_y, has_high_y = s > 0, s < ns - 1
    has_low_x, has_high_x = g > 0, g < ng - 1

    for i in range(nc + 2):
        a, b = edge_ya[i], edge_yb[i]
        low, high = jnp.where(odd_s, a, b), jnp.where(odd_s, b, a)
        if i == nc + 1:
            low, high = jnp.where(has_low_y, low, 0.0), jnp.where(has_high_y, high, 0.0)
        y_v[0, i] = low
        y_v[1, i] = high

    def side_x(i, high):
        if many_x == 1:
            return edge_x[0][i]
        return jnp.where(odd_g != high, edge_x[0][i], edge_x[1][i])

    row_hot, lane_hot = place_hots(loc[...], nx * ny)
    slot_hot = slot_hot_of(member[...], place[...], s)
    segments = own_press.shape[1]
    gathered = well_rows[...]
    found = [
        mat_hot(gathered, hot(iota((LANES, loc.shape[1]), 0) == seg[...] + (2 + k) * segments))
        for k in range(2)
    ]
    p_seg = jnp.sum(jnp.concatenate(found, axis=0) * slot_hot, axis=0, keepdims=True)
    push = strength[...] * (pcell[...] - p_seg)
    flows = jnp.concatenate(
        [
            jnp.where(lane_hot, jnp.maximum(push, 0.0), 0.0),
            jnp.where(lane_hot, jnp.minimum(push, 0.0), 0.0),
        ],
        axis=0,
    )
    spread = hot_mat_nt(hot(row_hot), flows, 2)

    own = jnp.sum(gathered, axis=0, keepdims=True)
    well_p = own_press[...]
    rate = own[:, segments : 2 * segments] - (well_p - 1.0) * own[:, :segments]
    order_hot = hot(iota((segments, segments), 0) == order[...])
    both = mat_hot(jnp.concatenate([rate, well_p], axis=0), order_hot)
    upper = hot(iota((segments, segments), 0) <= iota((segments, segments), 1))
    running = mat_hot(both[0:1], upper)
    press_ord = both[1:2]
    after = hot(iota((segments, segments), 0) == iota((segments, segments), 1) + 1)
    last = iota((1, segments), 1) == segments - 1
    nexts = jnp.where(last, exit_press[0], mat_hot(press_ord, after))
    res_ord = press_ord - nexts - friction[0] * running * jnp.abs(running)
    well_out[...] = sum(mat_nt(piece, order_hot) for piece in pieces_of(res_ord, 3))

    lane = iota((ny, LANES), 1)
    row = iota((ny, LANES), 0)
    first, final = row == 0, row == ny - 1

    def const(k):
        return jnp.concatenate([consts[k]] * (ny // SUBLANES), axis=0)

    stores = []
    for x in range(nx):
        rows = pl.ds(x * ny, ny)
        p_a, k_a = press[rows], perm[rows]
        twice_k = 2.0 * k_a

        def face(p_b, k_b, axis):
            t = const(nc + axis) * (twice_k * k_b) * inverse(k_a + k_b)
            flow = t * (p_a - p_b)
            return jnp.maximum(flow, 0.0), jnp.minimum(flow, 0.0)

        def other_x(field, i, high):
            at = x + 1 if high else x - 1
            return field[pl.ds(at * ny, ny)] if 0 <= at < nx else side_x(i, high)

        def other_y(field, i, high):
            if high:
                return jnp.where(final, y_v[1, i, pl.ds(x, 1)], pltpu.roll(field, ny - 1, 0))
            return jnp.where(first, y_v[0, i, pl.ds(x, 1)], pltpu.roll(field, 1, 0))

        centre = pore[rows] * jnp.where(flag[rows] == 1, const(nc + 4), const(nc + 3))
        centre += spread[x * ny : (x + 1) * ny, :LANES]
        ins = []
        for high in (True, False):
            p_b, k_b = other_x(press, nc, high), other_x(perm, nc + 1, high)
            if x == nx - 1 and high:
                k_b = jnp.where(has_high_x, k_b, 0.0)
            if x == 0 and not high:
                k_b = jnp.where(has_low_x, k_b, 0.0)
            ins.append(face(p_b, k_b, 0))
        for high in (True, False):
            ins.append(face(other_y(p_a, nc, high), other_y(k_a, nc + 1, high), 1))
        for shift, edge in ((LANES - 1, LANES - 1), (1, 0)):
            k_b = jnp.where(lane == edge, 0.0, pltpu.roll(k_a, shift, 1))
            ins.append(face(pltpu.roll(p_a, shift, 1), k_b, 2))
        for out, _ in ins:
            centre += out
        ins = [into for _, into in ins]
        pushed = mob[rows] * spread[x * ny : (x + 1) * ny, LANES:]
        for i in range(nc):
            base = MARGIN + x * ny
            c = carried[i, pl.ds(base, ny)]
            value = centre * c - old[i, rows] + const(i) * pushed
            for k, high in ((0, True), (1, False)):
                at = x + 1 if high else x - 1
                inside = 0 <= at < nx
                c_b = carried[i, pl.ds(MARGIN + at * ny, ny)] if inside else side_x(i, high)
                value += ins[k] * c_b
            up, down = carried[i, pl.ds(base + 1, ny)], carried[i, pl.ds(base - 1, ny)]
            value += ins[2] * jnp.where(final, y_v[1, i, pl.ds(x, 1)], up)
            value += ins[3] * jnp.where(first, y_v[0, i, pl.ds(x, 1)], down)
            value += ins[4] * pltpu.roll(c, LANES - 1, 1)
            value += ins[5] * pltpu.roll(c, 1, 1)
            res_v[i, rows] = value
        copy = pltpu.make_async_copy(res_v.at[:, rows], resid_out.at[:, rows], out_sems.at[x])
        copy.start()
        stores.append(copy)
    for copy in stores:
        copy.wait()


def swaps_of(count, other):
    pairs = [(i, i + 1) for i in range(1 if other else 0, count - 1, 2)]
    return pairs + [(b, a) for a, b in pairs]


def other_swaps_of(groups, count):
    swaps = [(g * count + a, g * count + b) for g in range(groups) for a, b in swaps_of(count, True)]
    ends = [(g * count + e, (g ^ 1) * count + e) for g in range(groups) for e in (0, count - 1)]
    return sorted(swaps + ends)


def per_device(
    amount,
    press,
    heat,
    flag,
    perm,
    pore,
    old,
    trans,
    visc,
    crit,
    attract,
    covol,
    slope,
    coupling,
    inject,
    locale,
    member,
    seg,
    strength,
    place,
    order,
    seg_press,
    exit_press,
    friction,
):
    axes = ("grp", "sub")
    nc, nx, ny, nz = amount.shape
    ng, ns = lax.axis_size("grp"), lax.axis_size("sub")
    rows = nx * ny
    perfs = locale.shape[0]
    wells, segments = place.shape[1], seg_press.shape[1]
    flat = lambda a: a.reshape(a.shape[:-3] + (rows, nz))
    line = lambda a: a.reshape(1, perfs)
    vm = pl.BlockSpec(memory_space=pltpu.VMEM)
    sm = pl.BlockSpec(memory_space=pltpu.SMEM)
    hbm = pl.BlockSpec(memory_space=pltpu.HBM)
    many_x = 1 if ng == 2 else 2

    amount, old = flat(amount), flat(old)
    press, heat, flag, perm, pore = (flat(a) for a in (press, heat, flag, perm, pore))
    locale, member, seg, strength = (line(a) for a in (locale, member, seg, strength))

    sources = (
        coupling, crit, attract, slope, covol, heat, press, locale, member, place,
        flag, visc, trans, inject, seg, strength, seg_press, perm,
    )
    kept = [
        pltpu.SMEM(a.shape, a.dtype) if a.ndim == 1 else pltpu.VMEM(a.shape, a.dtype)
        for a in sources
    ]
    in_hbm = lambda a: pltpu.with_memory_space_constraint(a, pltpu.HBM)

    lnphi, carried, mob, edge_x, edge_ya, edge_yb, part, pcell, consts = pl.pallas_call(
        functools.partial(phase_kernel, nx, ny, axes),
        out_shape=(
            jax.ShapeDtypeStruct((nc, rows, nz), BF16),
            jax.ShapeDtypeStruct((nc, rows + 2 * MARGIN, nz), F32),
            jax.ShapeDtypeStruct((rows, nz), F32),
            jax.ShapeDtypeStruct((many_x, nc + 2, ny, nz), F32),
            jax.ShapeDtypeStruct((nc + 2 + wells // 2 // nx, nx, nz), F32),
            jax.ShapeDtypeStruct((nc + 2, nx, nz), F32),
            jax.ShapeDtypeStruct((wells // 2, LANES), F32),
            jax.ShapeDtypeStruct((1, perfs), F32),
            jax.ShapeDtypeStruct((nc + 8, SUBLANES, LANES), F32),
        ),
        in_specs=[hbm] * (1 + len(sources)),
        out_specs=(hbm,) + (vm,) * 8,
        scratch_shapes=[
            *kept,
            pltpu.VMEM((nc, rows, nz), F32),
            pltpu.VMEM((3 * nc * ny, nx * nz), BF16),
            pltpu.VMEM((nc, rows, nz), F32),
            pltpu.VMEM((nc, rows, nz), BF16),
            pltpu.VMEM((4, rows, nz), F32),
            pltpu.VMEM((3, rows, nz), F32),
            pltpu.VMEM((3, nc, SUBLANES, LANES), F32),
            pltpu.SemaphoreType.DMA((len(sources),)),
            pltpu.SemaphoreType.DMA((2,)),
            pltpu.SemaphoreType.DMA((2,)),
        ],
        compiler_params=pltpu.CompilerParams(vmem_limit_bytes=VMEM_LIMIT),
        name="phase",
    )(in_hbm(amount), *(in_hbm(a) for a in sources))

    got_ya = lax.ppermute(edge_ya, "sub", swaps_of(ns, False))
    got_x = [lax.ppermute(edge_x[k], "grp", swaps_of(ng, k == 1)) for k in range(many_x)]
    got_yb = lax.ppermute(edge_yb, axes, other_swaps_of(ng, ns))
    part = part + got_ya[nc + 2 :].reshape(part.shape)
    same_parity = [list(range(ns - 1 - k, -1, -2)) for k in range(2)]
    well_rows = lax.all_to_all(
        part, "sub", split_axis=0, concat_axis=0, axis_index_groups=same_parity, tiled=True
    )

    resid, well = pl.pallas_call(
        functools.partial(flux_kernel, nx, ny, axes, many_x),
        out_shape=(
            jax.ShapeDtypeStruct((nc, rows, nz), F32),
            jax.ShapeDtypeStruct((1, segments), F32),
        ),
        in_specs=[vm] * 19 + [sm] * 2 + [vm] * many_x,
        out_specs=(hbm, vm),
        scratch_shapes=[
            pltpu.VMEM((2, nc + 2, nx, nz), F32),
            pltpu.VMEM((nc, rows, nz), F32),
            pltpu.SemaphoreType.DMA((nx,)),
        ],
        compiler_params=pltpu.CompilerParams(vmem_limit_bytes=VMEM_LIMIT),
        name="flux",
    )(
        carried, press, perm, pore, flag, old, mob, got_ya, got_yb, well_rows,
        locale, member, seg, strength, place, pcell,
        consts, seg_press, order, exit_press, friction, *got_x,
    )
    block = (nc, nx, ny, nz)
    return resid.reshape(block), lnphi.reshape(block), well


def solution(mesh):
    cells, parts = P("grp", "sub", None), P(None, "grp", "sub", None)
    listed = P(("grp", "sub"))
    row = P(("grp", "sub"), None)
    in_specs = (
        (parts,) + (cells,) * 5 + (parts,) + (P(),) * 8
        + (listed, row, listed, listed, P("grp", None), row, row, listed, listed)
    )
    return jax.shard_map(
        per_device, mesh=mesh, in_specs=in_specs, out_specs=(parts, parts, row), check_vma=False
    )
```

profile of v0, /device:TPU:0, one launch (start us, length us, event | category | flops | bytes accessed | tf_op | source)
XLA Modules:
  0.0 22.1 jit_solution(10394751010042531152)
XLA Ops:
  0.6 0.0 copy-start.10
  0.6 0.0 copy-start.9
  0.7 0.0 copy-start.8
  0.7 0.0 copy-start.7
  0.7 0.0 copy-start.6
  0.7 0.0 copy-start.5
  0.7 0.0 copy-start.3
  0.7 0.0 copy-start.2
  0.7 0.0 copy-start.1
  0.7 0.0 copy-start.11
  0.7 0.0 copy-start
  0.7 0.0 copy-start.4
  0.8 4.4 %phase.1 = (bf16[16,128,128]{2,1,0:T(8,128)(2,1)}, f32[16,144,128]{2,1,0:T(8,128)S(1)}, f32[128,128]{1,0:T(8,128)S(1)}, f32[1,18,16,128]{3,2,1,0:T(8,128)S(1)}, ...) custom-call(f32[16,128,128]{2,1,0:T(8,128)} %bitcast.40, ...), custom_call_target="tpu_custom_call" | custom-call | tf_op jit(solution)/shard_map/phase/pallas_call | solution.py:505
  5.1 0.5 %collective-permute-start = (f32[19,8,128]{2,1,0:T(8,128)S(1)}, f32[19,8,128]{2,1,0:T(8,128)S(1)}, u32[]{:S(2)}, u32[]{:S(2)}) collective-permute-start(f32[19,8,128]{2,1,0:T(8,128)S(1)} %get-tuple-element.16), channel_id=1, source_target_pairs={{0,1},{2,3},{4,5},{6,7},{8,9},{10,11},{12,13},{14,15},{1,0},{3,2},... | collective-permute-start | bytes 233480 | tf_op jit(solution)/shard_map/ppermute | solution.py:537
  5.7 2.6 %collective-permute-start.1 = (f32[18,8,128]{2,1,0:T(8,128)S(1)}, f32[18,8,128]{2,1,0:T(8,128)S(1)}, u32[]{:S(2)}, u32[]{:S(2)}) collective-permute-start(f32[18,8,128]{2,1,0:T(8,128)S(1)} %get-tuple-element.17), channel_id=1, source_target_pairs={{0,16},{1,2},{2,1},{3,4},{4,3},{5,6},{6,5},{7,8},{8,7},{9,10},{10,... | collective-permute-start | bytes 221192 | tf_op jit(solution)/shard_map/ppermute | solution.py:539
  8.2 0.1 collective-permute-start.2
  8.3 0.0 collective-permute-done.edge_ya
  8.3 0.6 %fusion = f32[8,128]{1,0:T(8,128)} fusion(f32[8,128]{1,0:T(8,128)S(1)} %get-tuple-element.18, f32[19,8,128]{2,1,0:T(8,128)S(1)} %collective-permute-done.edge_ya), kind=kLoop, calls=%fused_computation.1 | loop fusion | flops 1024 | bytes 12288 | tf_op jit(solution)/shard_map/add | solution.py:540
  8.9 8.3 %all-to-all-start = ((f32[8,1,128]{2,1,0:T(1,128)}), f32[8,1,128]{2,1,0:T(1,128)S(1)}, u32[]{:S(2)}, u32[]{:S(2)}) async-start(f32[8,1,128]{2,1,0:T(1,128)} %bitcast.13), calls=%async_computation | async-start | bytes 8192 | tf_op jit(solution)/shard_map/all_to_all | solution.py:542
  18.5 0.0 collective-permute-done.1.edge_yb
  18.5 0.9 %all-to-all-done = f32[8,1,128]{2,1,0:T(1,128)S(1)} async-done(((f32[8,1,128]{2,1,0:T(1,128)}), f32[8,1,128]{2,1,0:T(1,128)S(1)}, u32[]{:S(2)}, u32[]{:S(2)}) %all-to-all-start) | async-done | bytes 4128 | tf_op jit(solution)/shard_map/all_to_all | solution.py:542
  19.4 0.0 collective-permute-done.2.rest_0_
  19.4 0.0 copy-done.10
  19.4 0.0 copy-done.9
  19.4 0.0 copy-done.8
  19.4 0.0 copy-done.7
  19.4 0.0 copy-done.6
  19.4 0.0 copy-done.5
  19.4 0.0 copy-done.3
  19.4 0.0 copy-done.2
  19.5 0.0 copy-done.1
  19.5 0.0 copy-done.11
  19.5 0.0 copy-done
  19.5 0.0 copy-done.4
  19.5 2.6 %flux.1 = (f32[16,128,128]{2,1,0:T(8,128)}, f32[1,32]{1,0:T(1,128)}) custom-call(f32[16,144,128]{2,1,0:T(8,128)S(1)} %get-tuple-element.14.carried, f32[128,128]{1,0:T(8,128)S(1)} %bitcast.24, f32[128,128]{1,0:T(8,128)S(1)} %bitcast.28, f32[128,128]{1,0:T(8,128)S(1)} %bitcast.29, s32[128,128]{1,0:T(8,128)S(1)} %bitcast.26, f32[16,128,128]{2,1,0:T(8,128)S(1)} %bitcast.22, ...), custom_call_target="tpu_custom_call" | custom-call | tf_op jit(solution)/shard_map/flux/pallas_call | solution.py:546
Async XLA Ops:
  0.6 18.8 %copy-start.10 = (f32[1,32]{1,0:T(1,128)S(1)}, f32[1,32]{1,0:T(1,128)}, u32[]{:S(2)}) copy-start(f32[1,32]{1,0:T(1,128)} %own_press.1) | copy-start | bytes 388
  0.6 18.7 %copy-start.9 = (s32[1,16]{1,0:T(1,128)S(1)}, s32[1,16]{1,0:T(1,128)}, u32[]{:S(2)}) copy-start(s32[1,16]{1,0:T(1,128)} %place.1) | copy-start | bytes 196
  0.7 18.7 %copy-start.8 = (f32[256]{0:T(256)S(1)}, f32[256]{0:T(256)}, u32[]{:S(2)}) copy-start(f32[256]{0:T(256)} %param.42) | copy-start | bytes 3076
  0.7 18.7 %copy-start.7 = (s32[256]{0:T(256)S(1)}, s32[256]{0:T(256)}, u32[]{:S(2)}) copy-start(s32[256]{0:T(256)} %param.41) | copy-start | bytes 3076
  0.7 18.7 %copy-start.6 = (s32[256,1]{0,1:T(1,128)S(1)}, s32[256,1]{0,1:T(1,128)}, u32[]{:S(2)}) copy-start(s32[256,1]{0,1:T(1,128)} %param.40) | copy-start | bytes 3076
  0.7 18.7 %copy-start.5 = (s32[256]{0:T(256)S(1)}, s32[256]{0:T(256)}, u32[]{:S(2)}) copy-start(s32[256]{0:T(256)} %param.39) | copy-start | bytes 3076
  0.7 18.7 %copy-start.3 = (f32[8,16,128]{2,1,0:T(8,128)S(1)}, f32[8,16,128]{2,1,0:T(8,128)}, u32[]{:S(2)}) copy-start(f32[8,16,128]{2,1,0:T(8,128)} %param.28) | copy-start | bytes 196612
  0.7 18.7 %copy-start.2 = (s32[8,16,128]{2,1,0:T(8,128)S(1)}, s32[8,16,128]{2,1,0:T(8,128)}, u32[]{:S(2)}) copy-start(s32[8,16,128]{2,1,0:T(8,128)} %param.27) | copy-start | bytes 196612
  0.7 18.7 %copy-start.1 = (f32[8,16,128]{2,1,0:T(8,128)S(1)}, f32[8,16,128]{2,1,0:T(8,128)}, u32[]{:S(2)}) copy-start(f32[8,16,128]{2,1,0:T(8,128)} %param.25) | copy-start | bytes 196612
  0.7 18.7 %copy-start.11 = (s32[1,32]{1,0:T(1,128)S(1)}, s32[1,32]{1,0:T(1,128)}, u32[]{:S(2)}) copy-start(s32[1,32]{1,0:T(1,128)} %order.1) | copy-start | bytes 388
  0.7 18.7 %copy-start = (f32[16,8,16,128]{3,2,1,0:T(8,128)S(1)}, f32[16,8,16,128]{3,2,1,0:T(8,128)}, u32[]{:S(2)}) copy-start(f32[16,8,16,128]{3,2,1,0:T(8,128)} %param.30) | copy-start | bytes 3145732
  0.7 18.7 %copy-start.4 = (f32[8,16,128]{2,1,0:T(8,128)S(1)}, f32[8,16,128]{2,1,0:T(8,128)}, u32[]{:S(2)}) copy-start(f32[8,16,128]{2,1,0:T(8,128)} %param.29) | copy-start | bytes 196612
  5.1 3.2 %collective-permute-start = (f32[19,8,128]{2,1,0:T(8,128)S(1)}, f32[19,8,128]{2,1,0:T(8,128)S(1)}, u32[]{:S(2)}, u32[]{:S(2)}) collective-permute-start(f32[19,8,128]{2,1,0:T(8,128)S(1)} %get-tuple-element.16), channel_id=1, source_target_pairs={{0,1},{2,3},{4,5},{6,7},{8,9},{10,11},{12,13},{14,15},{1,0},{3,2},... | collective-permute-start | bytes 233480 | tf_op jit(solution)/shard_map/ppermute | solution.py:537
  5.7 12.8 %collective-permute-start.1 = (f32[18,8,128]{2,1,0:T(8,128)S(1)}, f32[18,8,128]{2,1,0:T(8,128)S(1)}, u32[]{:S(2)}, u32[]{:S(2)}) collective-permute-start(f32[18,8,128]{2,1,0:T(8,128)S(1)} %get-tuple-element.17), channel_id=1, source_target_pairs={{0,16},{1,2},{2,1},{3,4},{4,3},{5,6},{6,5},{7,8},{8,7},{9,10},{10,... | collective-permute-start | bytes 221192 | tf_op jit(solution)/shard_map/ppermute | solution.py:539
  8.2 11.2 %collective-permute-start.2 = (f32[18,16,128]{2,1,0:T(8,128)S(1)}, f32[18,16,128]{2,1,0:T(8,128)S(1)}, u32[]{:S(2)}, u32[]{:S(2)}) collective-permute-start(f32[18,16,128]{2,1,0:T(8,128)S(1)} %bitcast.39), channel_id=1, source_target_pairs={{0,16},{16,0},{1,17},{17,1},{2,18},{18,2},{3,19},{19,3},{4,20},{20... | collective-permute-start | bytes 442376 | tf_op jit(solution)/shard_map/ppermute | solution.py:538
  8.9 10.5 %all-to-all-start = ((f32[8,1,128]{2,1,0:T(1,128)}), f32[8,1,128]{2,1,0:T(1,128)S(1)}, u32[]{:S(2)}, u32[]{:S(2)}) async-start(f32[8,1,128]{2,1,0:T(1,128)} %bitcast.13), calls=%async_computation | async-start | bytes 8192 | tf_op jit(solution)/shard_map/all_to_all | solution.py:542
where the time goes:
time: 22.3 us; the launch traced here: 22.1 us
  starting transfers between devices  11.4 us (51%)
  Pallas kernels  7 us (31%)
  between operations  2.14 us (10%)
  waiting for transfers between devices  0.91 us (4%)
  other arithmetic  0.6 us (3%)
    all_to_all x1, starting transfers between devices, per_device(): lax.all_to_all(part, 'sub', split_axis=0, concat_axis=0, axis_index_group...  8.28 us
    pallas_call x1, Pallas kernels, per_device(): pl.pallas_call(functools.partial(phase_kernel, nx, ny, axes), out_shape=(...  4.38 us
    pallas_call x1, Pallas kernels, per_device(): pl.pallas_call(functools.partial(flux_kernel, nx, ny, axes, many_x), out_...  2.62 us
    ppermute x1, starting transfers between devices, per_device(): got_yb = lax.ppermute(edge_yb, axes, other_swaps_of(ng, ns))  2.56 us
    all_to_all x1, waiting for transfers between devices, per_device(): lax.all_to_all(part, 'sub', split_axis=0, concat_axis=0, axis_index_group...  0.9 us
    add x1, other arithmetic, per_device(): part = part + got_ya[nc + 2:].reshape(part.shape)  0.6 us
    ppermute x1, starting transfers between devices, per_device(): got_ya = lax.ppermute(edge_ya, 'sub', swaps_of(ns, False))  0.52 us
  transfers between devices with their start and end apart: 4, of which 1 were waited for; matrix products, arithmetic and copies ran while one was open for 3% of the time, Pallas kernels for 0%

commit v1 on v0

--- a/solution.py
+++ b/solution.py
@@ -47,10 +47,6 @@
     return sum(mat(piece, hot) for piece in pieces_of(x, count))
 
 
-def hot_mat_nt(hot, x, count=3):
-    return sum(mat_nt(hot, piece) for piece in pieces_of(x, count))
-
-
 def inverse(x):
     r = pl.reciprocal(x, approx=True)
     return r * (2.0 - x * r)
@@ -67,12 +63,9 @@
     return row_hot, lane_hot
 
 
-def slot_hot_of(member, place, own):
+def slot_hot_of(member, place):
     wells = place.shape[1]
-    half = wells // 2
-    row = iota((wells, wells), 0)
-    parity = jnp.where(row < half, own % 2, 1 - own % 2)
-    slot_of = hot(wells - 2 - 2 * (row % half) + parity == place)
+    slot_of = hot(iota((wells, wells), 0) == wells - 1 - place)
     member_hot = hot(iota((wells, member.shape[1]), 0) == member)
     return mat(slot_of, member_hot)
 
@@ -151,8 +144,7 @@
 
     p_cell = cells_of(press[...], 3)
     pcell_out[...] = p_cell
-    own_slot = lax.axis_index(axes[1])
-    slot_hot = slot_hot_of(member[...], place[...], own_slot).astype(BF16)
+    slot_hot = slot_hot_of(member[...], place[...])
     (heat,) = arrived("heat")
 
     shape3 = (ny // SUBLANES, SUBLANES, LANES)
@@ -230,18 +222,18 @@
     stores = []
     for x in range(nx):
         span = pl.ds(x * ny, ny)
-        e0, e1, e2, mr = (
-            a.reshape(shape3)
-            for a in (terms_v[0, span], terms_v[1, span], terms_v[2, span], field_v[3, span])
-        )
+        e0, e1, e2 = (terms_v[k, span].reshape(shape3) for k in range(3))
         for i in range(nc):
             value = table_v[2, i] * e1 - e0 - psi_v[i, span].reshape(shape3) * e2
             lnphi_v[i, span] = value.reshape(ny, LANES).astype(BF16)
-            carried = (mr * amount_v[i, span].reshape(shape3)).reshape(ny, LANES)
-            carried_out[i, pl.ds(MARGIN + x * ny, ny)] = carried
         if (x + 1) * 2 % nx == 0:
             span = pl.ds((x + 1 - nx // 2) * ny, nx // 2 * ny)
             stores.append(go(lnphi_v.at[:, span], lnphi_out.at[:, span], out_sems.at[len(stores)]))
+    for x in range(nx):
+        span = pl.ds(x * ny, ny)
+        mr = field_v[3, span]
+        for i in range(nc):
+            carried_out[i, pl.ds(MARGIN + x * ny, ny)] = mr * amount_v[i, span]
 
     total = sum(inject[i] for i in range(nc))
     share = 1.0 / jnp.full((SUBLANES, LANES), total, F32)
@@ -254,21 +246,17 @@
     seg, strength, own_press, perm = arrived("seg", "strength", "own_press", "perm")
     weight = strength[...] * cells_of(mob_out[...], 2)
     segments = own_press.shape[1]
-    place_of = iota((LANES, loc.shape[1]), 0)
-    sums = jnp.where(place_of == seg[...], weight, 0.0)
-    sums += jnp.where(place_of == seg[...] + segments, weight * (p_cell - 1.0), 0.0)
-    sums = hot_mat_nt(slot_hot, sums, 2)
-    half = sums.shape[0] // 2
-    for k in range(2):
-        shift = hot(iota((segments, LANES), 0) + (2 + k) * segments == iota((segments, LANES), 1))
-        with_press = sums[k * half : (k + 1) * half] + mat_hot(own_press[...], shift)
-        if k == 0:
-            part_out[...] = with_press
-        else:
-            edge_ya_out[pl.ds(nc + 2, half // nx)] = with_press.reshape(half // nx, nx, LANES)
+    lanes = iota((LANES, loc.shape[1]), 0)
+    shift = hot(iota((segments, LANES), 0) + 2 * segments == iota((segments, LANES), 1))
+    sums = mat_hot(own_press[...], shift)
+    for k, value in enumerate((weight, weight * (p_cell - 1.0))):
+        seg_hot = hot(lanes == seg[...] + k * segments)
+        for piece in pieces_of(slot_hot * value, 2):
+            sums += mat_nt(piece, seg_hot)
+    part_out[...] = sums
 
     odd_g = lax.axis_index(axes[0]) % 2 == 1
-    odd_s = own_slot % 2 == 1
+    odd_s = lax.axis_index(axes[1]) % 2 == 1
     for k in range(edge_x_out.shape[0]):
         at_low = odd_g if k == 0 else jnp.logical_not(odd_g)
         start = pl.multiple_of(jnp.where(at_low, 0, (nx - 1) * ny), ny)
@@ -338,23 +326,21 @@
         return jnp.where(odd_g != high, edge_x[0][i], edge_x[1][i])
 
     row_hot, lane_hot = place_hots(loc[...], nx * ny)
-    slot_hot = slot_hot_of(member[...], place[...], s)
+    slot_hot = slot_hot_of(member[...], place[...])
     segments = own_press.shape[1]
     gathered = well_rows[...]
-    found = [
-        mat_hot(gathered, hot(iota((LANES, loc.shape[1]), 0) == seg[...] + (2 + k) * segments))
-        for k in range(2)
-    ]
-    p_seg = jnp.sum(jnp.concatenate(found, axis=0) * slot_hot, axis=0, keepdims=True)
+    seg_hot = hot(iota((LANES, loc.shape[1]), 0) == seg[...] + 2 * segments)
+    p_seg = jnp.sum(mat_hot(gathered, seg_hot) * slot_hot, axis=0, keepdims=True)
     push = strength[...] * (pcell[...] - p_seg)
     flows = jnp.concatenate(
         [
-            jnp.where(lane_hot, jnp.maximum(push, 0.0), 0.0),
-            jnp.where(lane_hot, jnp.minimum(push, 0.0), 0.0),
+            jnp.where(row_hot, jnp.maximum(push, 0.0), 0.0),
+            jnp.where(row_hot, jnp.minimum(push, 0.0), 0.0),
         ],
         axis=0,
     )
-    spread = hot_mat_nt(hot(row_hot), flows, 2)
+    lane_hot = hot(lane_hot)
+    spread = sum(mat_nt(piece, lane_hot) for piece in pieces_of(flows, 2))
 
     own = jnp.sum(gathered, axis=0, keepdims=True)
     well_p = own_press[...]
@@ -398,7 +384,7 @@
             return jnp.where(first, y_v[0, i, pl.ds(x, 1)], pltpu.roll(field, 1, 0))
 
         centre = pore[rows] * jnp.where(flag[rows] == 1, const(nc + 4), const(nc + 3))
-        centre += spread[x * ny : (x + 1) * ny, :LANES]
+        centre += spread[x * ny : (x + 1) * ny]
         ins = []
         for high in (True, False):
             p_b, k_b = other_x(press, nc, high), other_x(perm, nc + 1, high)
@@ -415,7 +401,7 @@
         for out, _ in ins:
             centre += out
         ins = [into for _, into in ins]
-        pushed = mob[rows] * spread[x * ny : (x + 1) * ny, LANES:]
+        pushed = mob[rows] * spread[(nx + x) * ny : (nx + x + 1) * ny]
         for i in range(nc):
             base = MARGIN + x * ny
             c = carried[i, pl.ds(base, ny)]
@@ -509,9 +495,9 @@
             jax.ShapeDtypeStruct((nc, rows + 2 * MARGIN, nz), F32),
             jax.ShapeDtypeStruct((rows, nz), F32),
             jax.ShapeDtypeStruct((many_x, nc + 2, ny, nz), F32),
-            jax.ShapeDtypeStruct((nc + 2 + wells // 2 // nx, nx, nz), F32),
             jax.ShapeDtypeStruct((nc + 2, nx, nz), F32),
-            jax.ShapeDtypeStruct((wells // 2, LANES), F32),
+            jax.ShapeDtypeStruct((nc + 2, nx, nz), F32),
+            jax.ShapeDtypeStruct((wells, LANES), F32),
             jax.ShapeDtypeStruct((1, perfs), F32),
             jax.ShapeDtypeStruct((nc + 8, SUBLANES, LANES), F32),
         ),
@@ -537,10 +523,9 @@
     got_ya = lax.ppermute(edge_ya, "sub", swaps_of(ns, False))
     got_x = [lax.ppermute(edge_x[k], "grp", swaps_of(ng, k == 1)) for k in range(many_x)]
     got_yb = lax.ppermute(edge_yb, axes, other_swaps_of(ng, ns))
-    part = part + got_ya[nc + 2 :].reshape(part.shape)
-    same_parity = [list(range(ns - 1 - k, -1, -2)) for k in range(2)]
+    backward = [list(range(ns))[::-1]]
     well_rows = lax.all_to_all(
-        part, "sub", split_axis=0, concat_axis=0, axis_index_groups=same_parity, tiled=True
+        part, "sub", split_axis=0, concat_axis=0, axis_index_groups=backward, tiled=True
     )
 
     resid, well = pl.pallas_call(

time: 22.3 us -> 22.1 us (level)
  other arithmetic: 0.6 us -> 0 us
  Pallas kernels: 7 us -> 7.44 us
    ppermute x1, starting transfers between devices: 0.08 us -> 3 us  [per_device(): lax.ppermute(edge_x[k], 'grp', swaps_of(ng, k == 1))]
    ppermute x1, starting transfers between devices: 2.56 us -> 0.15 us  [per_device(): got_yb = lax.ppermute(edge_yb, axes, other_swaps_of(ng, ns))]
    pallas_call x1, Pallas kernels: 4.38 us -> 5 us  [per_device(): pl.pallas_call(functools.partial(phase_kernel, nx, ny, axes), out_shape=(...]
    add x1 -> x0, other arithmetic: 0.6 us -> none  [per_device(): part = part + got_ya[nc + 2:].reshape(part.shape)]
    ppermute x1, starting transfers between devices: 0.52 us -> 0.01 us  [per_device(): got_ya = lax.ppermute(edge_ya, 'sub', swaps_of(ns, False))]
  transfers between devices with their start and end apart: 4 -> 4, of which waited for: 1 -> 1; matrix products, arithmetic and copies ran while one was open for 3% -> 0% of each run, Pallas kernels for 0% -> 0%
where the time goes in v1:
time: 22.1 us; the launch traced here: 21.9 us
  starting transfers between devices  11.3 us (51%)
  Pallas kernels  7.44 us (34%)
  between operations  2.14 us (10%)
  waiting for transfers between devices  0.91 us (4%)
    all_to_all x1, starting transfers between devices, per_device(): lax.all_to_all(part, 'sub', split_axis=0, concat_axis=0, axis_index_group...  8.15 us
    pallas_call x1, Pallas kernels, per_device(): pl.pallas_call(functools.partial(phase_kernel, nx, ny, axes), out_shape=(...  5 us
    ppermute x1, starting transfers between devices, per_device(): lax.ppermute(edge_x[k], 'grp', swaps_of(ng, k == 1))  3 us
    pallas_call x1, Pallas kernels, per_device(): pl.pallas_call(functools.partial(flux_kernel, nx, ny, axes, many_x), out_...  2.44 us
    all_to_all x1, waiting for transfers between devices, per_device(): lax.all_to_all(part, 'sub', split_axis=0, concat_axis=0, axis_index_group...  0.9 us
  transfers between devices with their start and end apart: 4, of which 1 were waited for; matrix products, arithmetic and copies ran while one was open for 0% of the time, Pallas kernels for 0%

profile of v1, /device:TPU:0, one launch (start us, length us, event | category | flops | bytes accessed | tf_op | source)
XLA Modules:
  0.0 21.9 jit_solution(9712411521637181099)
XLA Ops:
  0.6 0.0 copy-start.10
  0.6 0.0 copy-start.9
  0.7 0.0 copy-start.8
  0.7 0.0 copy-start.7
  0.7 0.0 copy-start.6
  0.7 0.0 copy-start.5
  0.7 0.0 copy-start.3
  0.7 0.0 copy-start.2
  0.7 0.0 copy-start.1
  0.7 0.0 copy-start.11
  0.7 0.0 copy-start
  0.7 0.0 copy-start.4
  0.8 5.0 %phase.1 = (bf16[16,128,128]{2,1,0:T(8,128)(2,1)}, f32[16,144,128]{2,1,0:T(8,128)S(1)}, f32[128,128]{1,0:T(8,128)S(1)}, f32[1,18,16,128]{3,2,1,0:T(8,128)S(1)}, ...) custom-call(f32[16,128,128]{2,1,0:T(8,128)} %bitcast.36, ...), custom_call_target="tpu_custom_call" | custom-call | tf_op jit(solution)/shard_map/phase/pallas_call | solution.py:491
  5.8 3.0 %collective-permute-start.2 = (f32[18,16,128]{2,1,0:T(8,128)S(1)}, f32[18,16,128]{2,1,0:T(8,128)S(1)}, u32[]{:S(2)}, u32[]{:S(2)}) collective-permute-start(f32[18,16,128]{2,1,0:T(8,128)S(1)} %bitcast.35), channel_id=1, source_target_pairs={{0,16},{16,0},{1,17},{17,1},{2,18},{18,2},{3,19},{19,3},{4,20},{20... | collective-permute-start | bytes 442376 | tf_op jit(solution)/shard_map/ppermute | solution.py:524
  8.8 0.0 collective-permute-start
  8.8 0.2 collective-permute-start.1
  8.9 8.2 %all-to-all-start = ((f32[16,1,128]{2,1,0:T(1,128)}), f32[16,1,128]{2,1,0:T(1,128)S(1)}, u32[]{:S(2)}, u32[]{:S(2)}) async-start(f32[16,1,128]{2,1,0:T(1,128)} %bitcast.12), calls=%async_computation | async-start | bytes 16384 | tf_op jit(solution)/shard_map/all_to_all | solution.py:527
  18.4 0.9 %all-to-all-done = f32[16,1,128]{2,1,0:T(1,128)S(1)} async-done(((f32[16,1,128]{2,1,0:T(1,128)}), f32[16,1,128]{2,1,0:T(1,128)S(1)}, u32[]{:S(2)}, u32[]{:S(2)}) %all-to-all-start) | async-done | bytes 8224 | tf_op jit(solution)/shard_map/all_to_all | solution.py:527
  19.3 0.0 collective-permute-done.edge_ya
  19.3 0.0 collective-permute-done.1.edge_yb
  19.3 0.0 collective-permute-done.2.rest_0_
  19.3 0.0 copy-done.10
  19.3 0.0 copy-done.9
  19.3 0.0 copy-done.8
  19.3 0.0 copy-done.7
  19.3 0.0 copy-done.6
  19.3 0.0 copy-done.5
  19.4 0.0 copy-done.3
  19.4 0.0 copy-done.2
  19.4 0.0 copy-done.1
  19.4 0.0 copy-done.11
  19.4 0.0 copy-done
  19.4 0.0 copy-done.4
  19.4 2.4 %flux.1 = (f32[16,128,128]{2,1,0:T(8,128)}, f32[1,32]{1,0:T(1,128)}) custom-call(f32[16,144,128]{2,1,0:T(8,128)S(1)} %get-tuple-element.14.carried, f32[128,128]{1,0:T(8,128)S(1)} %bitcast.20, f32[128,128]{1,0:T(8,128)S(1)} %bitcast.24, f32[128,128]{1,0:T(8,128)S(1)} %bitcast.25, s32[128,128]{1,0:T(8,128)S(1)} %bitcast.22, f32[16,128,128]{2,1,0:T(8,128)S(1)} %bitcast.18, ...), custom_call_target="tpu_custom_call" | custom-call | tf_op jit(solution)/shard_map/flux/pallas_call | solution.py:531
Async XLA Ops:
  0.6 18.7 %copy-start.10 = (f32[1,32]{1,0:T(1,128)S(1)}, f32[1,32]{1,0:T(1,128)}, u32[]{:S(2)}) copy-start(f32[1,32]{1,0:T(1,128)} %own_press.1) | copy-start | bytes 388
  0.6 18.7 %copy-start.9 = (s32[1,16]{1,0:T(1,128)S(1)}, s32[1,16]{1,0:T(1,128)}, u32[]{:S(2)}) copy-start(s32[1,16]{1,0:T(1,128)} %place.1) | copy-start | bytes 196
  0.7 18.7 %copy-start.8 = (f32[256]{0:T(256)S(1)}, f32[256]{0:T(256)}, u32[]{:S(2)}) copy-start(f32[256]{0:T(256)} %param.42) | copy-start | bytes 3076
  0.7 18.7 %copy-start.7 = (s32[256]{0:T(256)S(1)}, s32[256]{0:T(256)}, u32[]{:S(2)}) copy-start(s32[256]{0:T(256)} %param.41) | copy-start | bytes 3076
  0.7 18.7 %copy-start.6 = (s32[256,1]{0,1:T(1,128)S(1)}, s32[256,1]{0,1:T(1,128)}, u32[]{:S(2)}) copy-start(s32[256,1]{0,1:T(1,128)} %param.40) | copy-start | bytes 3076
  0.7 18.7 %copy-start.5 = (s32[256]{0:T(256)S(1)}, s32[256]{0:T(256)}, u32[]{:S(2)}) copy-start(s32[256]{0:T(256)} %param.39) | copy-start | bytes 3076
  0.7 18.7 %copy-start.3 = (f32[8,16,128]{2,1,0:T(8,128)S(1)}, f32[8,16,128]{2,1,0:T(8,128)}, u32[]{:S(2)}) copy-start(f32[8,16,128]{2,1,0:T(8,128)} %param.28) | copy-start | bytes 196612
  0.7 18.7 %copy-start.2 = (s32[8,16,128]{2,1,0:T(8,128)S(1)}, s32[8,16,128]{2,1,0:T(8,128)}, u32[]{:S(2)}) copy-start(s32[8,16,128]{2,1,0:T(8,128)} %param.27) | copy-start | bytes 196612
  0.7 18.7 %copy-start.1 = (f32[8,16,128]{2,1,0:T(8,128)S(1)}, f32[8,16,128]{2,1,0:T(8,128)}, u32[]{:S(2)}) copy-start(f32[8,16,128]{2,1,0:T(8,128)} %param.25) | copy-start | bytes 196612
  0.7 18.7 %copy-start.11 = (s32[1,32]{1,0:T(1,128)S(1)}, s32[1,32]{1,0:T(1,128)}, u32[]{:S(2)}) copy-start(s32[1,32]{1,0:T(1,128)} %order.1) | copy-start | bytes 388
  0.7 18.7 %copy-start = (f32[16,8,16,128]{3,2,1,0:T(8,128)S(1)}, f32[16,8,16,128]{3,2,1,0:T(8,128)}, u32[]{:S(2)}) copy-start(f32[16,8,16,128]{3,2,1,0:T(8,128)} %param.30) | copy-start | bytes 3145732
  0.7 18.7 %copy-start.4 = (f32[8,16,128]{2,1,0:T(8,128)S(1)}, f32[8,16,128]{2,1,0:T(8,128)}, u32[]{:S(2)}) copy-start(f32[8,16,128]{2,1,0:T(8,128)} %param.29) | copy-start | bytes 196612
  5.8 13.5 %collective-permute-start.2 = (f32[18,16,128]{2,1,0:T(8,128)S(1)}, f32[18,16,128]{2,1,0:T(8,128)S(1)}, u32[]{:S(2)}, u32[]{:S(2)}) collective-permute-start(f32[18,16,128]{2,1,0:T(8,128)S(1)} %bitcast.35), channel_id=1, source_target_pairs={{0,16},{16,0},{1,17},{17,1},{2,18},{18,2},{3,19},{19,3},{4,20},{20... | collective-permute-start | bytes 442376 | tf_op jit(solution)/shard_map/ppermute | solution.py:524
  8.8 10.5 %collective-permute-start = (f32[18,8,128]{2,1,0:T(8,128)S(1)}, f32[18,8,128]{2,1,0:T(8,128)S(1)}, u32[]{:S(2)}, u32[]{:S(2)}) collective-permute-start(f32[18,8,128]{2,1,0:T(8,128)S(1)} %get-tuple-element.16), channel_id=1, source_target_pairs={{0,1},{2,3},{4,5},{6,7},{8,9},{10,11},{12,13},{14,15},{1,0},{3,2},... | collective-permute-start | bytes 221192 | tf_op jit(solution)/shard_map/ppermute | solution.py:523
  8.8 10.5 %collective-permute-start.1 = (f32[18,8,128]{2,1,0:T(8,128)S(1)}, f32[18,8,128]{2,1,0:T(8,128)S(1)}, u32[]{:S(2)}, u32[]{:S(2)}) collective-permute-start(f32[18,8,128]{2,1,0:T(8,128)S(1)} %get-tuple-element.17), channel_id=1, source_target_pairs={{0,16},{1,2},{2,1},{3,4},{4,3},{5,6},{6,5},{7,8},{8,7},{9,10},{10,... | collective-permute-start | bytes 221192 | tf_op jit(solution)/shard_map/ppermute | solution.py:525
  8.9 10.4 %all-to-all-start = ((f32[16,1,128]{2,1,0:T(1,128)}), f32[16,1,128]{2,1,0:T(1,128)S(1)}, u32[]{:S(2)}, u32[]{:S(2)}) async-start(f32[16,1,128]{2,1,0:T(1,128)} %bitcast.12), calls=%async_computation | async-start | bytes 16384 | tf_op jit(solution)/shard_map/all_to_all | solution.py:527

commit v2 on v1

--- a/solution.py
+++ b/solution.py
@@ -219,30 +219,6 @@
         terms_v[0, span] = jnp.log(z - big_b)
         terms_v[1, span] = (z - 1.0 + terms_v[1, span] * lb) * field_v[1, span]
         terms_v[2, span] = gr * lb
-    stores = []
-    for x in range(nx):
-        span = pl.ds(x * ny, ny)
-        e0, e1, e2 = (terms_v[k, span].reshape(shape3) for k in range(3))
-        for i in range(nc):
-            value = table_v[2, i] * e1 - e0 - psi_v[i, span].reshape(shape3) * e2
-            lnphi_v[i, span] = value.reshape(ny, LANES).astype(BF16)
-        if (x + 1) * 2 % nx == 0:
-            span = pl.ds((x + 1 - nx // 2) * ny, nx // 2 * ny)
-            stores.append(go(lnphi_v.at[:, span], lnphi_out.at[:, span], out_sems.at[len(stores)]))
-    for x in range(nx):
-        span = pl.ds(x * ny, ny)
-        mr = field_v[3, span]
-        for i in range(nc):
-            carried_out[i, pl.ds(MARGIN + x * ny, ny)] = mr * amount_v[i, span]
-
-    total = sum(inject[i] for i in range(nc))
-    share = 1.0 / jnp.full((SUBLANES, LANES), total, F32)
-    numbers = [trans[0], trans[1], trans[2], visc[0], visc[1]]
-    for i in range(nc):
-        consts_out[i] = inject[i] * share
-    for i, number in enumerate(numbers):
-        consts_out[nc + i] = jnp.full((SUBLANES, LANES), number, F32)
-
     seg, strength, own_press, perm = arrived("seg", "strength", "own_press", "perm")
     weight = strength[...] * cells_of(mob_out[...], 2)
     segments = own_press.shape[1]
@@ -254,6 +230,28 @@
         for piece in pieces_of(slot_hot * value, 2):
             sums += mat_nt(piece, seg_hot)
     part_out[...] = sums
+
+    total = sum(inject[i] for i in range(nc))
+    share = 1.0 / jnp.full((SUBLANES, LANES), total, F32)
+    numbers = [trans[0], trans[1], trans[2], visc[0], visc[1]]
+    for i in range(nc):
+        consts_out[i] = inject[i] * share
+    for i, number in enumerate(numbers):
+        consts_out[nc + i] = jnp.full((SUBLANES, LANES), number, F32)
+
+    stores = []
+    for x in range(nx):
+        span = pl.ds(x * ny, ny)
+        e0, e1, e2 = (terms_v[k, span].reshape(shape3) for k in range(3))
+        mr = field_v[3, span].reshape(shape3)
+        for i in range(nc):
+            value = table_v[2, i] * e1 - e0 - psi_v[i, span].reshape(shape3) * e2
+            lnphi_v[i, span] = value.reshape(ny, LANES).astype(BF16)
+            carried = (mr * amount_v[i, span].reshape(shape3)).reshape(ny, LANES)
+            carried_out[i, pl.ds(MARGIN + x * ny, ny)] = carried
+        if (x + 1) * 2 % nx == 0:
+            span = pl.ds((x + 1 - nx // 2) * ny, nx // 2 * ny)
+            stores.append(go(lnphi_v.at[:, span], lnphi_out.at[:, span], out_sems.at[len(stores)]))
 
     odd_g = lax.axis_index(axes[0]) % 2 == 1
     odd_s = lax.axis_index(axes[1]) % 2 == 1

time: 22.1 us -> 22.1 us (level)
  no operation moved by 1% of the time
where the time goes in v2:
time: 22.1 us; the launch traced here: 21.9 us
  starting transfers between devices  11.3 us (51%)
  Pallas kernels  7.43 us (34%)
  between operations  2.14 us (10%)
  waiting for transfers between devices  0.91 us (4%)
    all_to_all x1, starting transfers between devices, per_device(): lax.all_to_all(part, 'sub', split_axis=0, concat_axis=0, axis_index_group...  8.15 us
    pallas_call x1, Pallas kernels, per_device(): pl.pallas_call(functools.partial(phase_kernel, nx, ny, axes), out_shape=(...  4.99 us
    ppermute x1, starting transfers between devices, per_device(): lax.ppermute(edge_x[k], 'grp', swaps_of(ng, k == 1))  3 us
    pallas_call x1, Pallas kernels, per_device(): pl.pallas_call(functools.partial(flux_kernel, nx, ny, axes, many_x), out_...  2.44 us
    all_to_all x1, waiting for transfers between devices, per_device(): lax.all_to_all(part, 'sub', split_axis=0, concat_axis=0, axis_index_group...  0.9 us
  transfers between devices with their start and end apart: 4, of which 1 were waited for; matrix products, arithmetic and copies ran while one was open for 0% of the time, Pallas kernels for 0%

profile of v2, /device:TPU:0, one launch (start us, length us, event | category | flops | bytes accessed | tf_op | source)
XLA Modules:
  0.0 21.9 jit_solution(18374417517945761971)
XLA Ops:
  0.6 0.0 copy-start.10
  0.6 0.0 copy-start.9
  0.7 0.0 copy-start.8
  0.7 0.0 copy-start.7
  0.7 0.0 copy-start.6
  0.7 0.0 copy-start.5
  0.7 0.0 copy-start.3
  0.7 0.0 copy-start.2
  0.7 0.0 copy-start.1
  0.7 0.0 copy-start.11
  0.7 0.0 copy-start
  0.7 0.0 copy-start.4
  0.8 5.0 %phase.1 = (bf16[16,128,128]{2,1,0:T(8,128)(2,1)}, f32[16,144,128]{2,1,0:T(8,128)S(1)}, f32[128,128]{1,0:T(8,128)S(1)}, f32[1,18,16,128]{3,2,1,0:T(8,128)S(1)}, ...) custom-call(f32[16,128,128]{2,1,0:T(8,128)} %bitcast.36, ...), custom_call_target="tpu_custom_call" | custom-call | tf_op jit(solution)/shard_map/phase/pallas_call | solution.py:489
  5.8 3.0 %collective-permute-start.2 = (f32[18,16,128]{2,1,0:T(8,128)S(1)}, f32[18,16,128]{2,1,0:T(8,128)S(1)}, u32[]{:S(2)}, u32[]{:S(2)}) collective-permute-start(f32[18,16,128]{2,1,0:T(8,128)S(1)} %bitcast.35), channel_id=1, source_target_pairs={{0,16},{16,0},{1,17},{17,1},{2,18},{18,2},{3,19},{19,3},{4,20},{20... | collective-permute-start | bytes 442376 | tf_op jit(solution)/shard_map/ppermute | solution.py:522
  8.8 0.0 collective-permute-start
  8.8 0.2 collective-permute-start.1
  8.9 8.2 %all-to-all-start = ((f32[16,1,128]{2,1,0:T(1,128)}), f32[16,1,128]{2,1,0:T(1,128)S(1)}, u32[]{:S(2)}, u32[]{:S(2)}) async-start(f32[16,1,128]{2,1,0:T(1,128)} %bitcast.12), calls=%async_computation | async-start | bytes 16384 | tf_op jit(solution)/shard_map/all_to_all | solution.py:525
  18.4 0.9 %all-to-all-done = f32[16,1,128]{2,1,0:T(1,128)S(1)} async-done(((f32[16,1,128]{2,1,0:T(1,128)}), f32[16,1,128]{2,1,0:T(1,128)S(1)}, u32[]{:S(2)}, u32[]{:S(2)}) %all-to-all-start) | async-done | bytes 8224 | tf_op jit(solution)/shard_map/all_to_all | solution.py:525
  19.3 0.0 collective-permute-done.edge_ya
  19.3 0.0 collective-permute-done.1.edge_yb
  19.3 0.0 collective-permute-done.2.rest_0_
  19.3 0.0 copy-done.10
  19.3 0.0 copy-done.9
  19.3 0.0 copy-done.8
  19.3 0.0 copy-done.7
  19.3 0.0 copy-done.6
  19.3 0.0 copy-done.5
  19.4 0.0 copy-done.3
  19.4 0.0 copy-done.2
  19.4 0.0 copy-done.1
  19.4 0.0 copy-done.11
  19.4 0.0 copy-done
  19.4 0.0 copy-done.4
  19.4 2.4 %flux.1 = (f32[16,128,128]{2,1,0:T(8,128)}, f32[1,32]{1,0:T(1,128)}) custom-call(f32[16,144,128]{2,1,0:T(8,128)S(1)} %get-tuple-element.14.carried, f32[128,128]{1,0:T(8,128)S(1)} %bitcast.20, f32[128,128]{1,0:T(8,128)S(1)} %bitcast.24, f32[128,128]{1,0:T(8,128)S(1)} %bitcast.25, s32[128,128]{1,0:T(8,128)S(1)} %bitcast.22, f32[16,128,128]{2,1,0:T(8,128)S(1)} %bitcast.18, ...), custom_call_target="tpu_custom_call" | custom-call | tf_op jit(solution)/shard_map/flux/pallas_call | solution.py:529
Async XLA Ops:
  0.6 18.7 %copy-start.10 = (f32[1,32]{1,0:T(1,128)S(1)}, f32[1,32]{1,0:T(1,128)}, u32[]{:S(2)}) copy-start(f32[1,32]{1,0:T(1,128)} %own_press.1) | copy-start | bytes 388
  0.6 18.7 %copy-start.9 = (s32[1,16]{1,0:T(1,128)S(1)}, s32[1,16]{1,0:T(1,128)}, u32[]{:S(2)}) copy-start(s32[1,16]{1,0:T(1,128)} %place.1) | copy-start | bytes 196
  0.7 18.7 %copy-start.8 = (f32[256]{0:T(256)S(1)}, f32[256]{0:T(256)}, u32[]{:S(2)}) copy-start(f32[256]{0:T(256)} %param.42) | copy-start | bytes 3076
  0.7 18.7 %copy-start.7 = (s32[256]{0:T(256)S(1)}, s32[256]{0:T(256)}, u32[]{:S(2)}) copy-start(s32[256]{0:T(256)} %param.41) | copy-start | bytes 3076
  0.7 18.7 %copy-start.6 = (s32[256,1]{0,1:T(1,128)S(1)}, s32[256,1]{0,1:T(1,128)}, u32[]{:S(2)}) copy-start(s32[256,1]{0,1:T(1,128)} %param.40) | copy-start | bytes 3076
  0.7 18.7 %copy-start.5 = (s32[256]{0:T(256)S(1)}, s32[256]{0:T(256)}, u32[]{:S(2)}) copy-start(s32[256]{0:T(256)} %param.39) | copy-start | bytes 3076
  0.7 18.7 %copy-start.3 = (f32[8,16,128]{2,1,0:T(8,128)S(1)}, f32[8,16,128]{2,1,0:T(8,128)}, u32[]{:S(2)}) copy-start(f32[8,16,128]{2,1,0:T(8,128)} %param.28) | copy-start | bytes 196612
  0.7 18.7 %copy-start.2 = (s32[8,16,128]{2,1,0:T(8,128)S(1)}, s32[8,16,128]{2,1,0:T(8,128)}, u32[]{:S(2)}) copy-start(s32[8,16,128]{2,1,0:T(8,128)} %param.27) | copy-start | bytes 196612
  0.7 18.7 %copy-start.1 = (f32[8,16,128]{2,1,0:T(8,128)S(1)}, f32[8,16,128]{2,1,0:T(8,128)}, u32[]{:S(2)}) copy-start(f32[8,16,128]{2,1,0:T(8,128)} %param.25) | copy-start | bytes 196612
  0.7 18.7 %copy-start.11 = (s32[1,32]{1,0:T(1,128)S(1)}, s32[1,32]{1,0:T(1,128)}, u32[]{:S(2)}) copy-start(s32[1,32]{1,0:T(1,128)} %order.1) | copy-start | bytes 388
  0.7 18.7 %copy-start = (f32[16,8,16,128]{3,2,1,0:T(8,128)S(1)}, f32[16,8,16,128]{3,2,1,0:T(8,128)}, u32[]{:S(2)}) copy-start(f32[16,8,16,128]{3,2,1,0:T(8,128)} %param.30) | copy-start | bytes 3145732
  0.7 18.7 %copy-start.4 = (f32[8,16,128]{2,1,0:T(8,128)S(1)}, f32[8,16,128]{2,1,0:T(8,128)}, u32[]{:S(2)}) copy-start(f32[8,16,128]{2,1,0:T(8,128)} %param.29) | copy-start | bytes 196612
  5.8 13.5 %collective-permute-start.2 = (f32[18,16,128]{2,1,0:T(8,128)S(1)}, f32[18,16,128]{2,1,0:T(8,128)S(1)}, u32[]{:S(2)}, u32[]{:S(2)}) collective-permute-start(f32[18,16,128]{2,1,0:T(8,128)S(1)} %bitcast.35), channel_id=1, source_target_pairs={{0,16},{16,0},{1,17},{17,1},{2,18},{18,2},{3,19},{19,3},{4,20},{20... | collective-permute-start | bytes 442376 | tf_op jit(solution)/shard_map/ppermute | solution.py:522
  8.8 10.5 %collective-permute-start = (f32[18,8,128]{2,1,0:T(8,128)S(1)}, f32[18,8,128]{2,1,0:T(8,128)S(1)}, u32[]{:S(2)}, u32[]{:S(2)}) collective-permute-start(f32[18,8,128]{2,1,0:T(8,128)S(1)} %get-tuple-element.16), channel_id=1, source_target_pairs={{0,1},{2,3},{4,5},{6,7},{8,9},{10,11},{12,13},{14,15},{1,0},{3,2},... | collective-permute-start | bytes 221192 | tf_op jit(solution)/shard_map/ppermute | solution.py:521
  8.8 10.5 %collective-permute-start.1 = (f32[18,8,128]{2,1,0:T(8,128)S(1)}, f32[18,8,128]{2,1,0:T(8,128)S(1)}, u32[]{:S(2)}, u32[]{:S(2)}) collective-permute-start(f32[18,8,128]{2,1,0:T(8,128)S(1)} %get-tuple-element.17), channel_id=1, source_target_pairs={{0,16},{1,2},{2,1},{3,4},{4,3},{5,6},{6,5},{7,8},{8,7},{9,10},{10,... | collective-permute-start | bytes 221192 | tf_op jit(solution)/shard_map/ppermute | solution.py:523
  8.9 10.4 %all-to-all-start = ((f32[16,1,128]{2,1,0:T(1,128)}), f32[16,1,128]{2,1,0:T(1,128)S(1)}, u32[]{:S(2)}, u32[]{:S(2)}) async-start(f32[16,1,128]{2,1,0:T(1,128)} %bitcast.12), calls=%async_computation | async-start | bytes 16384 | tf_op jit(solution)/shard_map/all_to_all | solution.py:525

commit v3 on v2

--- a/solution.py
+++ b/solution.py
@@ -18,7 +18,7 @@
 MARGIN = 8
 WHOLE = (
     "coupling", "crit", "attract", "slope", "covol", "heat", "press", "loc", "member", "place",
-    "flag", "visc", "trans", "inject", "seg", "strength", "own_press", "perm",
+    "flag", "visc", "trans", "inject", "seg", "strength", "own_press", "perm", "pore",
 )
 
 
@@ -79,18 +79,21 @@
 ):
     sources, rest = rest[: len(WHOLE)], rest[len(WHOLE) :]
     (
-        lnphi_out,
+        psi_v,
+        terms_v,
         carried_out,
         mob_out,
+        store_out,
         edge_x_out,
         edge_ya_out,
         edge_yb_out,
         part_out,
         pcell_out,
         consts_out,
-    ) = rest[:9]
-    targets, rest = rest[9 : 9 + len(WHOLE)], rest[9 + len(WHOLE) :]
-    amount_v, split_v, psi_v, lnphi_v, field_v, terms_v, table_v, small_sems, in_sems, out_sems = rest
+        covol_out,
+    ) = rest[:12]
+    targets, rest = rest[12 : 12 + len(WHOLE)], rest[12 + len(WHOLE) :]
+    amount_v, split_v, field_v, table_v, part_v, small_sems, in_sems, out_sems = rest
     nc = amount.shape[0]
     per = 2
     chunks = nx // per
@@ -229,29 +232,24 @@
         seg_hot = hot(lanes == seg[...] + k * segments)
         for piece in pieces_of(slot_hot * value, 2):
             sums += mat_nt(piece, seg_hot)
-    part_out[...] = sums
+    part_v[...] = sums
+    part_copy = go(part_v, part_out, out_sems.at[0])
+
+    (pore,) = arrived("pore")
+    store_out[...] = pore[...] * jnp.where(flag[...] == 1, visc[1], visc[0])
+    for x in range(nx):
+        span = pl.ds(x * ny, ny)
+        mr = field_v[3, span]
+        for i in range(nc):
+            carried_out[i, pl.ds(MARGIN + x * ny, ny)] = mr * amount_v[i, span]
 
     total = sum(inject[i] for i in range(nc))
     share = 1.0 / jnp.full((SUBLANES, LANES), total, F32)
-    numbers = [trans[0], trans[1], trans[2], visc[0], visc[1]]
     for i in range(nc):
         consts_out[i] = inject[i] * share
-    for i, number in enumerate(numbers):
-        consts_out[nc + i] = jnp.full((SUBLANES, LANES), number, F32)
-
-    stores = []
-    for x in range(nx):
-        span = pl.ds(x * ny, ny)
-        e0, e1, e2 = (terms_v[k, span].reshape(shape3) for k in range(3))
-        mr = field_v[3, span].reshape(shape3)
-        for i in range(nc):
-            value = table_v[2, i] * e1 - e0 - psi_v[i, span].reshape(shape3) * e2
-            lnphi_v[i, span] = value.reshape(ny, LANES).astype(BF16)
-            carried = (mr * amount_v[i, span].reshape(shape3)).reshape(ny, LANES)
-            carried_out[i, pl.ds(MARGIN + x * ny, ny)] = carried
-        if (x + 1) * 2 % nx == 0:
-            span = pl.ds((x + 1 - nx // 2) * ny, nx // 2 * ny)
-            stores.append(go(lnphi_v.at[:, span], lnphi_out.at[:, span], out_sems.at[len(stores)]))
+        covol_out[pl.ds(i, 1)] = jnp.full((1, LANES), covol[i], F32)
+    for k in range(3):
+        consts_out[nc + k] = jnp.full((SUBLANES, LANES), trans[k], F32)
 
     odd_g = lax.axis_index(axes[0]) % 2 == 1
     odd_s = lax.axis_index(axes[1]) % 2 == 1
@@ -269,6 +267,24 @@
         high = source[pl.ds(skip + ny - 1, nx, stride=ny)]
         edge_ya_out[i] = jnp.where(odd_s, low, high)
         edge_yb_out[i] = jnp.where(odd_s, high, low)
+    part_copy.wait()
+
+
+def fugacity_kernel(ny, psi, terms, covol, lnphi_out, lnphi_v, sems):
+    nc, rows, _ = psi.shape
+    parts = sems.shape[0]
+    stores = []
+    for part in range(parts):
+        for x in range(part * rows // parts // ny, (part + 1) * rows // parts // ny):
+            span = pl.ds(x * ny, ny)
+            e0, e1, e2 = (terms[k, span] for k in range(3))
+            for i in range(nc):
+                value = covol[pl.ds(i, 1)] * e1 - e0 - psi[i, span] * e2
+                lnphi_v[i, span] = value.astype(BF16)
+        span = pl.ds(part * rows // parts, rows // parts)
+        copy = pltpu.make_async_copy(lnphi_v.at[:, span], lnphi_out.at[:, span], sems.at[part])
+        copy.start()
+        stores.append(copy)
     for copy in stores:
         copy.wait()
 
@@ -281,9 +297,8 @@
     carried,
     press,
     perm,
-    pore,
-    flag,
-    old,
+    store,
+    old_in,
     mob,
     edge_ya,
     edge_yb,
@@ -302,8 +317,14 @@
     *rest,
 ):
     edge_x, rest = rest[:many_x], rest[many_x:]
-    resid_out, well_out, y_v, res_v, out_sems = rest
+    resid_out, well_out, old, y_v, res_v, well_v, in_sems, out_sems = rest
     nc = carried.shape[0]
+    loads = []
+    for x in range(nx):
+        span = pl.ds(x * ny, ny)
+        copy = pltpu.make_async_copy(old_in.at[:, span], old.at[:, span], in_sems.at[x])
+        copy.start()
+        loads.append(copy)
     g, s = lax.axis_index(axes[0]), lax.axis_index(axes[1])
     ng, ns = lax.axis_size(axes[0]), lax.axis_size(axes[1])
     odd_g, odd_s = g % 2 == 1, s % 2 == 1
@@ -352,7 +373,9 @@
     last = iota((1, segments), 1) == segments - 1
     nexts = jnp.where(last, exit_press[0], mat_hot(press_ord, after))
     res_ord = press_ord - nexts - friction[0] * running * jnp.abs(running)
-    well_out[...] = sum(mat_nt(piece, order_hot) for piece in pieces_of(res_ord, 3))
+    well_v[...] = sum(mat_nt(piece, order_hot) for piece in pieces_of(res_ord, 3))
+    stores = [pltpu.make_async_copy(well_v, well_out, out_sems.at[nx])]
+    stores[0].start()
 
     lane = iota((ny, LANES), 1)
     row = iota((ny, LANES), 0)
@@ -361,7 +384,6 @@
     def const(k):
         return jnp.concatenate([consts[k]] * (ny // SUBLANES), axis=0)
 
-    stores = []
     for x in range(nx):
         rows = pl.ds(x * ny, ny)
         p_a, k_a = press[rows], perm[rows]
@@ -381,8 +403,7 @@
                 return jnp.where(final, y_v[1, i, pl.ds(x, 1)], pltpu.roll(field, ny - 1, 0))
             return jnp.where(first, y_v[0, i, pl.ds(x, 1)], pltpu.roll(field, 1, 0))
 
-        centre = pore[rows] * jnp.where(flag[rows] == 1, const(nc + 4), const(nc + 3))
-        centre += spread[x * ny : (x + 1) * ny]
+        centre = store[rows] + spread[x * ny : (x + 1) * ny]
         ins = []
         for high in (True, False):
             p_b, k_b = other_x(press, nc, high), other_x(perm, nc + 1, high)
@@ -400,6 +421,7 @@
             centre += out
         ins = [into for _, into in ins]
         pushed = mob[rows] * spread[(nx + x) * ny : (nx + x + 1) * ny]
+        loads[x].wait()
         for i in range(nc):
             base = MARGIN + x * ny
             c = carried[i, pl.ds(base, ny)]
@@ -478,7 +500,7 @@
 
     sources = (
         coupling, crit, attract, slope, covol, heat, press, locale, member, place,
-        flag, visc, trans, inject, seg, strength, seg_press, perm,
+        flag, visc, trans, inject, seg, strength, seg_press, perm, pore,
     )
     kept = [
         pltpu.SMEM(a.shape, a.dtype) if a.ndim == 1 else pltpu.VMEM(a.shape, a.dtype)
@@ -486,33 +508,34 @@
     ]
     in_hbm = lambda a: pltpu.with_memory_space_constraint(a, pltpu.HBM)
 
-    lnphi, carried, mob, edge_x, edge_ya, edge_yb, part, pcell, consts = pl.pallas_call(
+    psi, terms, carried, mob, store, edge_x, edge_ya, edge_yb, part, pcell, consts, covols = pl.pallas_call(
         functools.partial(phase_kernel, nx, ny, axes),
         out_shape=(
-            jax.ShapeDtypeStruct((nc, rows, nz), BF16),
+            jax.ShapeDtypeStruct((nc, rows, nz), F32),
+            jax.ShapeDtypeStruct((3, rows, nz), F32),
             jax.ShapeDtypeStruct((nc, rows + 2 * MARGIN, nz), F32),
+            jax.ShapeDtypeStruct((rows, nz), F32),
             jax.ShapeDtypeStruct((rows, nz), F32),
             jax.ShapeDtypeStruct((many_x, nc + 2, ny, nz), F32),
             jax.ShapeDtypeStruct((nc + 2, nx, nz), F32),
             jax.ShapeDtypeStruct((nc + 2, nx, nz), F32),
             jax.ShapeDtypeStruct((wells, LANES), F32),
             jax.ShapeDtypeStruct((1, perfs), F32),
-            jax.ShapeDtypeStruct((nc + 8, SUBLANES, LANES), F32),
+            jax.ShapeDtypeStruct((nc + 3, SUBLANES, LANES), F32),
+            jax.ShapeDtypeStruct((nc, LANES), F32),
         ),
         in_specs=[hbm] * (1 + len(sources)),
-        out_specs=(hbm,) + (vm,) * 8,
+        out_specs=(vm,) * 8 + (hbm,) + (vm,) * 3,
         scratch_shapes=[
             *kept,
             pltpu.VMEM((nc, rows, nz), F32),
             pltpu.VMEM((3 * nc * ny, nx * nz), BF16),
-            pltpu.VMEM((nc, rows, nz), F32),
-            pltpu.VMEM((nc, rows, nz), BF16),
             pltpu.VMEM((4, rows, nz), F32),
-            pltpu.VMEM((3, rows, nz), F32),
             pltpu.VMEM((3, nc, SUBLANES, LANES), F32),
+            pltpu.VMEM((wells, LANES), F32),
             pltpu.SemaphoreType.DMA((len(sources),)),
             pltpu.SemaphoreType.DMA((2,)),
-            pltpu.SemaphoreType.DMA((2,)),
+            pltpu.SemaphoreType.DMA((1,)),
         ],
         compiler_params=pltpu.CompilerParams(vmem_limit_bytes=VMEM_LIMIT),
         name="phase",
@@ -526,23 +549,39 @@
         part, "sub", split_axis=0, concat_axis=0, axis_index_groups=backward, tiled=True
     )
 
+    lnphi = pl.pallas_call(
+        functools.partial(fugacity_kernel, ny),
+        out_shape=jax.ShapeDtypeStruct((nc, rows, nz), BF16),
+        in_specs=[vm] * 3,
+        out_specs=hbm,
+        scratch_shapes=[pltpu.VMEM((nc, rows, nz), BF16), pltpu.SemaphoreType.DMA((4,))],
+        compiler_params=pltpu.CompilerParams(vmem_limit_bytes=VMEM_LIMIT),
+        cost_estimate=pl.CostEstimate(
+            flops=8 * nc * rows * nz, bytes_accessed=256 * nc * rows * nz, transcendentals=0
+        ),
+        name="fugacity",
+    )(psi, terms, covols)
+
     resid, well = pl.pallas_call(
         functools.partial(flux_kernel, nx, ny, axes, many_x),
         out_shape=(
             jax.ShapeDtypeStruct((nc, rows, nz), F32),
             jax.ShapeDtypeStruct((1, segments), F32),
         ),
-        in_specs=[vm] * 19 + [sm] * 2 + [vm] * many_x,
-        out_specs=(hbm, vm),
+        in_specs=[vm] * 4 + [hbm] + [vm] * 13 + [sm] * 2 + [vm] * many_x,
+        out_specs=(hbm, hbm),
         scratch_shapes=[
+            pltpu.VMEM((nc, rows, nz), F32),
             pltpu.VMEM((2, nc + 2, nx, nz), F32),
             pltpu.VMEM((nc, rows, nz), F32),
+            pltpu.VMEM((1, segments), F32),
             pltpu.SemaphoreType.DMA((nx,)),
+            pltpu.SemaphoreType.DMA((nx + 1,)),
         ],
         compiler_params=pltpu.CompilerParams(vmem_limit_bytes=VMEM_LIMIT),
         name="flux",
     )(
-        carried, press, perm, pore, flag, old, mob, got_ya, got_yb, well_rows,
+        carried, press, perm, store, in_hbm(old), mob, got_ya, got_yb, well_rows,
         locale, member, seg, strength, place, pcell,
         consts, seg_press, order, exit_press, friction, *got_x,
     )

time: 22.1 us -> 22.1 us (level)
  Pallas kernels: 7.43 us -> 8.33 us
  waiting for transfers between devices: 0.91 us -> 0.04 us
    all_to_all x1, waiting for transfers between devices: 0.9 us -> 0.03 us  [per_device(): lax.all_to_all(part, 'sub', split_axis=0, concat_axis=0, axis_index_group...]
    pallas_call x0 -> x1, Pallas kernels: none -> 0.86 us  [per_device(): pl.pallas_call(functools.partial(fugacity_kernel, ny), out_shape=jax.Shap...]
    pallas_call x1, Pallas kernels: 2.44 us -> 3.07 us  [per_device(): pl.pallas_call(functools.partial(flux_kernel, nx, ny, axes, many_x), out_...]
    pallas_call x1, Pallas kernels: 4.99 us -> 4.39 us  [per_device(): pl.pallas_call(functools.partial(phase_kernel, nx, ny, axes), out_shape=(...]
  transfers between devices with their start and end apart: 4 -> 4, of which waited for: 1 -> 0; matrix products, arithmetic and copies ran while one was open for 0% -> 0% of each run, Pallas kernels for 0% -> 4%
where the time goes in v3:
time: 22.1 us; the launch traced here: 21.8 us
  starting transfers between devices  11.3 us (51%)
  Pallas kernels  8.33 us (38%)
  between operations  2.1 us (10%)
    all_to_all x1, starting transfers between devices, per_device(): lax.all_to_all(part, 'sub', split_axis=0, concat_axis=0, axis_index_group...  8.15 us
    pallas_call x1, Pallas kernels, per_device(): pl.pallas_call(functools.partial(phase_kernel, nx, ny, axes), out_shape=(...  4.39 us
    pallas_call x1, Pallas kernels, per_device(): pl.pallas_call(functools.partial(flux_kernel, nx, ny, axes, many_x), out_...  3.07 us
    ppermute x1, starting transfers between devices, per_device(): lax.ppermute(edge_x[k], 'grp', swaps_of(ng, k == 1))  3 us
    pallas_call x1, Pallas kernels, per_device(): pl.pallas_call(functools.partial(fugacity_kernel, ny), out_shape=jax.Shap...  0.86 us
  transfers between devices with their start and end apart: 4, of which 0 were waited for; matrix products, arithmetic and copies ran while one was open for 0% of the time, Pallas kernels for 4%

profile of v3, /device:TPU:0, one launch (start us, length us, event | category | flops | bytes accessed | tf_op | source)
XLA Modules:
  0.0 21.8 jit_solution(13007483757340618495)
XLA Ops:
  0.6 4.4 %phase.1 = (f32[16,128,128]{2,1,0:T(8,128)S(1)}, f32[3,128,128]{2,1,0:T(8,128)S(1)}, f32[16,144,128]{2,1,0:T(8,128)S(1)}, f32[128,128]{1,0:T(8,128)S(1)}, f32[12...) custom-call(f32[16,128,128]{2,1,0:T(8,128)} %bitcast.33, ...), custom_call_target="tpu_custom_call" | custom-call | tf_op jit(solution)/shard_map/phase/pallas_call | solution.py:511
  5.0 0.0 copy-start
  5.0 0.0 copy-start.1
  5.1 0.0 copy-start.2
  5.1 0.0 copy-start.3
  5.1 0.0 copy-start.4
  5.1 0.0 copy-start.5
  5.1 0.0 copy-start.6
  5.1 0.0 copy-start.7
  5.1 0.0 copy-start.8
  5.1 3.0 %collective-permute-start.2 = (f32[18,16,128]{2,1,0:T(8,128)S(1)}, f32[18,16,128]{2,1,0:T(8,128)S(1)}, u32[]{:S(2)}, u32[]{:S(2)}) collective-permute-start(f32[18,16,128]{2,1,0:T(8,128)S(1)} %bitcast.31), channel_id=1, source_target_pairs={{0,16},{16,0},{1,17},{17,1},{2,18},{18,2},{3,19},{19,3},{4,20},{20... | collective-permute-start | bytes 442376 | tf_op jit(solution)/shard_map/ppermute | solution.py:545
  8.1 0.0 collective-permute-start
  8.1 0.2 collective-permute-start.1
  8.3 8.2 %all-to-all-start = ((f32[16,1,128]{2,1,0:T(1,128)}), f32[16,1,128]{2,1,0:T(1,128)S(1)}, u32[]{:S(2)}, u32[]{:S(2)}) async-start(f32[16,1,128]{2,1,0:T(1,128)} %bitcast.12), calls=%async_computation | async-start | bytes 16384 | tf_op jit(solution)/shard_map/all_to_all | solution.py:548
  17.8 0.9 %fugacity.1 = bf16[16,128,128]{2,1,0:T(8,128)(2,1)} custom-call(f32[16,128,128]{2,1,0:T(8,128)S(1)} %get-tuple-element.27.psi, f32[3,128,128]{2,1,0:T(8,128)S(1)} %get-tuple-element.28.terms, f32[16,128]{1,0:T(8,128)S(1)} %get-tuple-element.29.covol), custom_call_target="tpu_custom_call" | custom-call | flops 2097152 | bytes 67108864 | tf_op jit(solution)/shard_map/fugacity/pallas_call | solution.py:552
  18.6 0.0 all-to-all-done
  18.7 0.0 collective-permute-done.edge_ya
  18.7 0.0 collective-permute-done.1.edge_yb
  18.7 0.0 collective-permute-done.2.rest_0_
  18.7 0.0 copy-done
  18.7 0.0 copy-done.1
  18.7 0.0 copy-done.2
  18.7 0.0 copy-done.3
  18.7 0.0 copy-done.4
  18.7 0.0 copy-done.5
  18.7 0.0 copy-done.6
  18.7 0.0 copy-done.7
  18.7 0.0 copy-done.8
  18.8 3.1 %flux.1 = (f32[16,128,128]{2,1,0:T(8,128)}, f32[1,32]{1,0:T(1,128)}) custom-call(f32[16,144,128]{2,1,0:T(8,128)S(1)} %get-tuple-element.17.carried, f32[128,128]{1,0:T(8,128)S(1)} %bitcast.19, f32[128,128]{1,0:T(8,128)S(1)} %bitcast.21, f32[128,128]{1,0:T(8,128)S(1)} %get-tuple-element.18.store, f32[16,128,128]{2,1,0:T(8,128)} %bitcast.32, ...), custom_call_target="tpu_custom_call" | custom-call | tf_op jit(solution)/shard_map/flux/pallas_call | solution.py:565
Async XLA Ops:
  5.0 13.6 %copy-start = (f32[8,16,128]{2,1,0:T(8,128)S(1)}, f32[8,16,128]{2,1,0:T(8,128)}, u32[]{:S(2)}) copy-start(f32[8,16,128]{2,1,0:T(8,128)} %param.25) | copy-start | bytes 196612
  5.0 13.6 %copy-start.1 = (f32[8,16,128]{2,1,0:T(8,128)S(1)}, f32[8,16,128]{2,1,0:T(8,128)}, u32[]{:S(2)}) copy-start(f32[8,16,128]{2,1,0:T(8,128)} %param.28) | copy-start | bytes 196612
  5.1 13.6 %copy-start.2 = (s32[256]{0:T(256)S(1)}, s32[256]{0:T(256)}, u32[]{:S(2)}) copy-start(s32[256]{0:T(256)} %param.39) | copy-start | bytes 3076
  5.1 13.6 %copy-start.3 = (s32[256,1]{0,1:T(1,128)S(1)}, s32[256,1]{0,1:T(1,128)}, u32[]{:S(2)}) copy-start(s32[256,1]{0,1:T(1,128)} %param.40) | copy-start | bytes 3076
  5.1 13.6 %copy-start.4 = (s32[256]{0:T(256)S(1)}, s32[256]{0:T(256)}, u32[]{:S(2)}) copy-start(s32[256]{0:T(256)} %param.41) | copy-start | bytes 3076
  5.1 13.6 %copy-start.5 = (f32[256]{0:T(256)S(1)}, f32[256]{0:T(256)}, u32[]{:S(2)}) copy-start(f32[256]{0:T(256)} %param.42) | copy-start | bytes 3076
  5.1 13.6 %copy-start.6 = (s32[1,16]{1,0:T(1,128)S(1)}, s32[1,16]{1,0:T(1,128)}, u32[]{:S(2)}) copy-start(s32[1,16]{1,0:T(1,128)} %place.1) | copy-start | bytes 196
  5.1 13.6 %copy-start.7 = (f32[1,32]{1,0:T(1,128)S(1)}, f32[1,32]{1,0:T(1,128)}, u32[]{:S(2)}) copy-start(f32[1,32]{1,0:T(1,128)} %own_press.1) | copy-start | bytes 388
  5.1 13.6 %copy-start.8 = (s32[1,32]{1,0:T(1,128)S(1)}, s32[1,32]{1,0:T(1,128)}, u32[]{:S(2)}) copy-start(s32[1,32]{1,0:T(1,128)} %order.1) | copy-start | bytes 388
  5.1 13.5 %collective-permute-start.2 = (f32[18,16,128]{2,1,0:T(8,128)S(1)}, f32[18,16,128]{2,1,0:T(8,128)S(1)}, u32[]{:S(2)}, u32[]{:S(2)}) collective-permute-start(f32[18,16,128]{2,1,0:T(8,128)S(1)} %bitcast.31), channel_id=1, source_target_pairs={{0,16},{16,0},{1,17},{17,1},{2,18},{18,2},{3,19},{19,3},{4,20},{20... | collective-permute-start | bytes 442376 | tf_op jit(solution)/shard_map/ppermute | solution.py:545
  8.1 10.5 %collective-permute-start = (f32[18,8,128]{2,1,0:T(8,128)S(1)}, f32[18,8,128]{2,1,0:T(8,128)S(1)}, u32[]{:S(2)}, u32[]{:S(2)}) collective-permute-start(f32[18,8,128]{2,1,0:T(8,128)S(1)} %get-tuple-element.20), channel_id=1, source_target_pairs={{0,1},{2,3},{4,5},{6,7},{8,9},{10,11},{12,13},{14,15},{1,0},{3,2},... | collective-permute-start | bytes 221192 | tf_op jit(solution)/shard_map/ppermute | solution.py:544
  8.1 10.5 %collective-permute-start.1 = (f32[18,8,128]{2,1,0:T(8,128)S(1)}, f32[18,8,128]{2,1,0:T(8,128)S(1)}, u32[]{:S(2)}, u32[]{:S(2)}) collective-permute-start(f32[18,8,128]{2,1,0:T(8,128)S(1)} %get-tuple-element.21), channel_id=1, source_target_pairs={{0,16},{1,2},{2,1},{3,4},{4,3},{5,6},{6,5},{7,8},{8,7},{9,10},{10,... | collective-permute-start | bytes 221192 | tf_op jit(solution)/shard_map/ppermute | solution.py:546
  8.3 10.4 %all-to-all-start = ((f32[16,1,128]{2,1,0:T(1,128)}), f32[16,1,128]{2,1,0:T(1,128)S(1)}, u32[]{:S(2)}, u32[]{:S(2)}) async-start(f32[16,1,128]{2,1,0:T(1,128)} %bitcast.12), calls=%async_computation | async-start | bytes 16384 | tf_op jit(solution)/shard_map/all_to_all | solution.py:548

commit v4 on v3

--- a/solution.py
+++ b/solution.py
@@ -147,7 +147,7 @@
 
     p_cell = cells_of(press[...], 3)
     pcell_out[...] = p_cell
-    slot_hot = slot_hot_of(member[...], place[...])
+    slot_hot = slot_hot_of(member[...], place[...]).astype(BF16)
     (heat,) = arrived("heat")
 
     shape3 = (ny // SUBLANES, SUBLANES, LANES)
@@ -227,11 +227,10 @@
     segments = own_press.shape[1]
     lanes = iota((LANES, loc.shape[1]), 0)
     shift = hot(iota((segments, LANES), 0) + 2 * segments == iota((segments, LANES), 1))
-    sums = mat_hot(own_press[...], shift)
-    for k, value in enumerate((weight, weight * (p_cell - 1.0))):
-        seg_hot = hot(lanes == seg[...] + k * segments)
-        for piece in pieces_of(slot_hot * value, 2):
-            sums += mat_nt(piece, seg_hot)
+    sums = jnp.where(lanes == seg[...], weight, 0.0)
+    sums += jnp.where(lanes == seg[...] + segments, weight * (p_cell - 1.0), 0.0)
+    sums = sum(mat_nt(slot_hot, piece) for piece in pieces_of(sums, 2))
+    sums += mat_hot(own_press[...], shift)
     part_v[...] = sums
     part_copy = go(part_v, part_out, out_sems.at[0])
 
@@ -325,6 +324,12 @@
         copy = pltpu.make_async_copy(old_in.at[:, span], old.at[:, span], in_sems.at[x])
         copy.start()
         loads.append(copy)
+
+    def send(x):
+        rows = pl.ds(x * ny, ny)
+        copy = pltpu.make_async_copy(res_v.at[:, rows], resid_out.at[:, rows], out_sems.at[x])
+        copy.start()
+        stores.append(copy)
     g, s = lax.axis_index(axes[0]), lax.axis_index(axes[1])
     ng, ns = lax.axis_size(axes[0]), lax.axis_size(axes[1])
     odd_g, odd_s = g % 2 == 1, s % 2 == 1
@@ -421,11 +426,20 @@
             centre += out
         ins = [into for _, into in ins]
         pushed = mob[rows] * spread[(nx + x) * ny : (nx + x + 1) * ny]
-        loads[x].wait()
+        if x == nx // 2:
+            for load in loads:
+                load.wait()
+            for before in range(x):
+                span = pl.ds(before * ny, ny)
+                for i in range(nc):
+                    res_v[i, span] = res_v[i, span] - old[i, span]
+                send(before)
         for i in range(nc):
             base = MARGIN + x * ny
             c = carried[i, pl.ds(base, ny)]
-            value = centre * c - old[i, rows] + const(i) * pushed
+            value = centre * c + const(i) * pushed
+            if x >= nx // 2:
+                value -= old[i, rows]
             for k, high in ((0, True), (1, False)):
                 at = x + 1 if high else x - 1
                 inside = 0 <= at < nx
@@ -437,9 +451,8 @@
             value += ins[4] * pltpu.roll(c, LANES - 1, 1)
             value += ins[5] * pltpu.roll(c, 1, 1)
             res_v[i, rows] = value
-        copy = pltpu.make_async_copy(res_v.at[:, rows], resid_out.at[:, rows], out_sems.at[x])
-        copy.start()
-        stores.append(copy)
+        if x >= nx // 2:
+            send(x)
     for copy in stores:
         copy.wait()
 

time: 22.1 us -> 22.1 us (level)
  no operation moved by 1% of the time
where the time goes in v4:
time: 22.1 us; the launch traced here: 21.8 us
  starting transfers between devices  11.3 us (51%)
  Pallas kernels  8.31 us (38%)
  between operations  2.1 us (10%)
    all_to_all x1, starting transfers between devices, per_device(): lax.all_to_all(part, 'sub', split_axis=0, concat_axis=0, axis_index_group...  8.15 us
    pallas_call x1, Pallas kernels, per_device(): pl.pallas_call(functools.partial(phase_kernel, nx, ny, axes), out_shape=(...  4.37 us
    pallas_call x1, Pallas kernels, per_device(): pl.pallas_call(functools.partial(flux_kernel, nx, ny, axes, many_x), out_...  3.08 us
    ppermute x1, starting transfers between devices, per_device(): lax.ppermute(edge_x[k], 'grp', swaps_of(ng, k == 1))  3 us
    pallas_call x1, Pallas kernels, per_device(): pl.pallas_call(functools.partial(fugacity_kernel, ny), out_shape=jax.Shap...  0.86 us
  transfers between devices with their start and end apart: 4, of which 0 were waited for; matrix products, arithmetic and copies ran while one was open for 0% of the time, Pallas kernels for 4%

profile of v4, /device:TPU:0, one launch (start us, length us, event | category | flops | bytes accessed | tf_op | source)
XLA Modules:
  0.0 21.8 jit_solution(8022052164278132149)
XLA Ops:
  0.6 4.4 %phase.1 = (f32[16,128,128]{2,1,0:T(8,128)S(1)}, f32[3,128,128]{2,1,0:T(8,128)S(1)}, f32[16,144,128]{2,1,0:T(8,128)S(1)}, f32[128,128]{1,0:T(8,128)S(1)}, f32[12...) custom-call(f32[16,128,128]{2,1,0:T(8,128)} %bitcast.33, ...), custom_call_target="tpu_custom_call" | custom-call | tf_op jit(solution)/shard_map/phase/pallas_call | solution.py:524
  5.0 0.0 copy-start
  5.0 0.0 copy-start.1
  5.0 0.0 copy-start.2
  5.0 0.0 copy-start.3
  5.1 0.0 copy-start.4
  5.1 0.0 copy-start.5
  5.1 0.0 copy-start.6
  5.1 0.0 copy-start.7
  5.1 0.0 copy-start.8
  5.1 3.0 %collective-permute-start.2 = (f32[18,16,128]{2,1,0:T(8,128)S(1)}, f32[18,16,128]{2,1,0:T(8,128)S(1)}, u32[]{:S(2)}, u32[]{:S(2)}) collective-permute-start(f32[18,16,128]{2,1,0:T(8,128)S(1)} %bitcast.31), channel_id=1, source_target_pairs={{0,16},{16,0},{1,17},{17,1},{2,18},{18,2},{3,19},{19,3},{4,20},{20... | collective-permute-start | bytes 442376 | tf_op jit(solution)/shard_map/ppermute | solution.py:558
  8.1 0.0 collective-permute-start
  8.1 0.2 collective-permute-start.1
  8.3 8.2 %all-to-all-start = ((f32[16,1,128]{2,1,0:T(1,128)}), f32[16,1,128]{2,1,0:T(1,128)S(1)}, u32[]{:S(2)}, u32[]{:S(2)}) async-start(f32[16,1,128]{2,1,0:T(1,128)} %bitcast.12), calls=%async_computation | async-start | bytes 16384 | tf_op jit(solution)/shard_map/all_to_all | solution.py:561
  17.7 0.9 %fugacity.1 = bf16[16,128,128]{2,1,0:T(8,128)(2,1)} custom-call(f32[16,128,128]{2,1,0:T(8,128)S(1)} %get-tuple-element.27.psi, f32[3,128,128]{2,1,0:T(8,128)S(1)} %get-tuple-element.28.terms, f32[16,128]{1,0:T(8,128)S(1)} %get-tuple-element.29.covol), custom_call_target="tpu_custom_call" | custom-call | flops 2097152 | bytes 67108864 | tf_op jit(solution)/shard_map/fugacity/pallas_call | solution.py:565
  18.6 0.0 all-to-all-done
  18.6 0.0 collective-permute-done.edge_ya
  18.6 0.0 collective-permute-done.1.edge_yb
  18.6 0.0 collective-permute-done.2.rest_0_
  18.6 0.0 copy-done
  18.7 0.0 copy-done.1
  18.7 0.0 copy-done.2
  18.7 0.0 copy-done.3
  18.7 0.0 copy-done.4
  18.7 0.0 copy-done.5
  18.7 0.0 copy-done.6
  18.7 0.0 copy-done.7
  18.7 0.0 copy-done.8
  18.7 3.1 %flux.1 = (f32[16,128,128]{2,1,0:T(8,128)}, f32[1,32]{1,0:T(1,128)}) custom-call(f32[16,144,128]{2,1,0:T(8,128)S(1)} %get-tuple-element.17.carried, f32[128,128]{1,0:T(8,128)S(1)} %bitcast.19, f32[128,128]{1,0:T(8,128)S(1)} %bitcast.21, f32[128,128]{1,0:T(8,128)S(1)} %get-tuple-element.18.store, f32[16,128,128]{2,1,0:T(8,128)} %bitcast.32, ...), custom_call_target="tpu_custom_call" | custom-call | tf_op jit(solution)/shard_map/flux/pallas_call | solution.py:578
Async XLA Ops:
  5.0 13.6 %copy-start = (f32[8,16,128]{2,1,0:T(8,128)S(1)}, f32[8,16,128]{2,1,0:T(8,128)}, u32[]{:S(2)}) copy-start(f32[8,16,128]{2,1,0:T(8,128)} %param.25) | copy-start | bytes 196612
  5.0 13.6 %copy-start.1 = (f32[8,16,128]{2,1,0:T(8,128)S(1)}, f32[8,16,128]{2,1,0:T(8,128)}, u32[]{:S(2)}) copy-start(f32[8,16,128]{2,1,0:T(8,128)} %param.28) | copy-start | bytes 196612
  5.0 13.6 %copy-start.2 = (s32[256]{0:T(256)S(1)}, s32[256]{0:T(256)}, u32[]{:S(2)}) copy-start(s32[256]{0:T(256)} %param.39) | copy-start | bytes 3076
  5.0 13.6 %copy-start.3 = (s32[256,1]{0,1:T(1,128)S(1)}, s32[256,1]{0,1:T(1,128)}, u32[]{:S(2)}) copy-start(s32[256,1]{0,1:T(1,128)} %param.40) | copy-start | bytes 3076
  5.1 13.6 %copy-start.4 = (s32[256]{0:T(256)S(1)}, s32[256]{0:T(256)}, u32[]{:S(2)}) copy-start(s32[256]{0:T(256)} %param.41) | copy-start | bytes 3076
  5.1 13.6 %copy-start.5 = (f32[256]{0:T(256)S(1)}, f32[256]{0:T(256)}, u32[]{:S(2)}) copy-start(f32[256]{0:T(256)} %param.42) | copy-start | bytes 3076
  5.1 13.6 %copy-start.6 = (s32[1,16]{1,0:T(1,128)S(1)}, s32[1,16]{1,0:T(1,128)}, u32[]{:S(2)}) copy-start(s32[1,16]{1,0:T(1,128)} %place.1) | copy-start | bytes 196
  5.1 13.6 %copy-start.7 = (f32[1,32]{1,0:T(1,128)S(1)}, f32[1,32]{1,0:T(1,128)}, u32[]{:S(2)}) copy-start(f32[1,32]{1,0:T(1,128)} %own_press.1) | copy-start | bytes 388
  5.1 13.6 %copy-start.8 = (s32[1,32]{1,0:T(1,128)S(1)}, s32[1,32]{1,0:T(1,128)}, u32[]{:S(2)}) copy-start(s32[1,32]{1,0:T(1,128)} %order.1) | copy-start | bytes 388
  5.1 13.5 %collective-permute-start.2 = (f32[18,16,128]{2,1,0:T(8,128)S(1)}, f32[18,16,128]{2,1,0:T(8,128)S(1)}, u32[]{:S(2)}, u32[]{:S(2)}) collective-permute-start(f32[18,16,128]{2,1,0:T(8,128)S(1)} %bitcast.31), channel_id=1, source_target_pairs={{0,16},{16,0},{1,17},{17,1},{2,18},{18,2},{3,19},{19,3},{4,20},{20... | collective-permute-start | bytes 442376 | tf_op jit(solution)/shard_map/ppermute | solution.py:558
  8.1 10.5 %collective-permute-start = (f32[18,8,128]{2,1,0:T(8,128)S(1)}, f32[18,8,128]{2,1,0:T(8,128)S(1)}, u32[]{:S(2)}, u32[]{:S(2)}) collective-permute-start(f32[18,8,128]{2,1,0:T(8,128)S(1)} %get-tuple-element.20), channel_id=1, source_target_pairs={{0,1},{2,3},{4,5},{6,7},{8,9},{10,11},{12,13},{14,15},{1,0},{3,2},... | collective-permute-start | bytes 221192 | tf_op jit(solution)/shard_map/ppermute | solution.py:557
  8.1 10.5 %collective-permute-start.1 = (f32[18,8,128]{2,1,0:T(8,128)S(1)}, f32[18,8,128]{2,1,0:T(8,128)S(1)}, u32[]{:S(2)}, u32[]{:S(2)}) collective-permute-start(f32[18,8,128]{2,1,0:T(8,128)S(1)} %get-tuple-element.21), channel_id=1, source_target_pairs={{0,16},{1,2},{2,1},{3,4},{4,3},{5,6},{6,5},{7,8},{8,7},{9,10},{10,... | collective-permute-start | bytes 221192 | tf_op jit(solution)/shard_map/ppermute | solution.py:559
  8.3 10.4 %all-to-all-start = ((f32[16,1,128]{2,1,0:T(1,128)}), f32[16,1,128]{2,1,0:T(1,128)S(1)}, u32[]{:S(2)}, u32[]{:S(2)}) async-start(f32[16,1,128]{2,1,0:T(1,128)} %bitcast.12), calls=%async_computation | async-start | bytes 16384 | tf_op jit(solution)/shard_map/all_to_all | solution.py:561

commit v5 on v2

--- a/solution.py
+++ b/solution.py
@@ -90,7 +90,7 @@
         consts_out,
     ) = rest[:9]
     targets, rest = rest[9 : 9 + len(WHOLE)], rest[9 + len(WHOLE) :]
-    amount_v, split_v, psi_v, lnphi_v, field_v, terms_v, table_v, small_sems, in_sems, out_sems = rest
+    amount_v, split_v, psi_v, lnphi_v, field_v, terms_v, table_v, part_v, small_sems, in_sems, out_sems = rest
     nc = amount.shape[0]
     per = 2
     chunks = nx // per
@@ -229,7 +229,8 @@
         seg_hot = hot(lanes == seg[...] + k * segments)
         for piece in pieces_of(slot_hot * value, 2):
             sums += mat_nt(piece, seg_hot)
-    part_out[...] = sums
+    part_v[...] = sums
+    part_copy = go(part_v, part_out, out_sems.at[2])
 
     total = sum(inject[i] for i in range(nc))
     share = 1.0 / jnp.full((SUBLANES, LANES), total, F32)
@@ -269,7 +270,7 @@
         high = source[pl.ds(skip + ny - 1, nx, stride=ny)]
         edge_ya_out[i] = jnp.where(odd_s, low, high)
         edge_yb_out[i] = jnp.where(odd_s, high, low)
-    for copy in stores:
+    for copy in [part_copy, *stores]:
         copy.wait()
 
 
@@ -302,7 +303,7 @@
     *rest,
 ):
     edge_x, rest = rest[:many_x], rest[many_x:]
-    resid_out, well_out, y_v, res_v, out_sems = rest
+    resid_out, well_out, y_v, res_v, well_v, out_sems = rest
     nc = carried.shape[0]
     g, s = lax.axis_index(axes[0]), lax.axis_index(axes[1])
     ng, ns = lax.axis_size(axes[0]), lax.axis_size(axes[1])
@@ -352,7 +353,9 @@
     last = iota((1, segments), 1) == segments - 1
     nexts = jnp.where(last, exit_press[0], mat_hot(press_ord, after))
     res_ord = press_ord - nexts - friction[0] * running * jnp.abs(running)
-    well_out[...] = sum(mat_nt(piece, order_hot) for piece in pieces_of(res_ord, 3))
+    well_v[...] = sum(mat_nt(piece, order_hot) for piece in pieces_of(res_ord, 3))
+    stores = [pltpu.make_async_copy(well_v, well_out, out_sems.at[nx])]
+    stores[0].start()
 
     lane = iota((ny, LANES), 1)
     row = iota((ny, LANES), 0)
@@ -361,7 +364,6 @@
     def const(k):
         return jnp.concatenate([consts[k]] * (ny // SUBLANES), axis=0)
 
-    stores = []
     for x in range(nx):
         rows = pl.ds(x * ny, ny)
         p_a, k_a = press[rows], perm[rows]
@@ -500,7 +502,7 @@
             jax.ShapeDtypeStruct((nc + 8, SUBLANES, LANES), F32),
         ),
         in_specs=[hbm] * (1 + len(sources)),
-        out_specs=(hbm,) + (vm,) * 8,
+        out_specs=(hbm,) + (vm,) * 5 + (hbm,) + (vm,) * 2,
         scratch_shapes=[
             *kept,
             pltpu.VMEM((nc, rows, nz), F32),
@@ -510,9 +512,10 @@
             pltpu.VMEM((4, rows, nz), F32),
             pltpu.VMEM((3, rows, nz), F32),
             pltpu.VMEM((3, nc, SUBLANES, LANES), F32),
+            pltpu.VMEM((wells, LANES), F32),
             pltpu.SemaphoreType.DMA((len(sources),)),
             pltpu.SemaphoreType.DMA((2,)),
-            pltpu.SemaphoreType.DMA((2,)),
+            pltpu.SemaphoreType.DMA((3,)),
         ],
         compiler_params=pltpu.CompilerParams(vmem_limit_bytes=VMEM_LIMIT),
         name="phase",
@@ -533,11 +536,12 @@
             jax.ShapeDtypeStruct((1, segments), F32),
         ),
         in_specs=[vm] * 19 + [sm] * 2 + [vm] * many_x,
-        out_specs=(hbm, vm),
+        out_specs=(hbm, hbm),
         scratch_shapes=[
             pltpu.VMEM((2, nc + 2, nx, nz), F32),
             pltpu.VMEM((nc, rows, nz), F32),
-            pltpu.SemaphoreType.DMA((nx,)),
+            pltpu.VMEM((1, segments), F32),
+            pltpu.SemaphoreType.DMA((nx + 1,)),
         ],
         compiler_params=pltpu.CompilerParams(vmem_limit_bytes=VMEM_LIMIT),
         name="flux",

time: 22.1 us -> 21.7 us (0.982)
  Pallas kernels: 7.43 us -> 7.03 us
where the time goes in v5:
time: 21.7 us; the launch traced here: 21.5 us
  starting transfers between devices  11.3 us (52%)
  Pallas kernels  7.03 us (32%)
  between operations  2.14 us (10%)
  waiting for transfers between devices  0.91 us (4%)
    all_to_all x1, starting transfers between devices, per_device(): lax.all_to_all(part, 'sub', split_axis=0, concat_axis=0, axis_index_group...  8.16 us
    pallas_call x1, Pallas kernels, per_device(): pl.pallas_call(functools.partial(phase_kernel, nx, ny, axes), out_shape=(...  4.81 us
    ppermute x1, starting transfers between devices, per_device(): lax.ppermute(edge_x[k], 'grp', swaps_of(ng, k == 1))  3 us
    pallas_call x1, Pallas kernels, per_device(): pl.pallas_call(functools.partial(flux_kernel, nx, ny, axes, many_x), out_...  2.23 us
    all_to_all x1, waiting for transfers between devices, per_device(): lax.all_to_all(part, 'sub', split_axis=0, concat_axis=0, axis_index_group...  0.9 us
  transfers between devices with their start and end apart: 4, of which 1 were waited for; matrix products, arithmetic and copies ran while one was open for 0% of the time, Pallas kernels for 0%

profile of v5, /device:TPU:0, one launch (start us, length us, event | category | flops | bytes accessed | tf_op | source)
XLA Modules:
  0.0 21.5 jit_solution(12606455153249947850)
XLA Ops:
  0.6 0.0 copy-start.10
  0.6 0.0 copy-start.9
  0.7 0.0 copy-start.8
  0.7 0.0 copy-start.7
  0.7 0.0 copy-start.6
  0.7 0.0 copy-start.5
  0.7 0.0 copy-start.3
  0.7 0.0 copy-start.2
  0.7 0.0 copy-start.1
  0.7 0.0 copy-start.11
  0.7 0.0 copy-start
  0.7 0.0 copy-start.4
  0.8 4.8 %phase.1 = (bf16[16,128,128]{2,1,0:T(8,128)(2,1)}, f32[16,144,128]{2,1,0:T(8,128)S(1)}, f32[128,128]{1,0:T(8,128)S(1)}, f32[1,18,16,128]{3,2,1,0:T(8,128)S(1)}, ...) custom-call(f32[16,128,128]{2,1,0:T(8,128)} %bitcast.36, ...), custom_call_target="tpu_custom_call" | custom-call | tf_op jit(solution)/shard_map/phase/pallas_call | solution.py:491
  5.6 3.0 %collective-permute-start.2 = (f32[18,16,128]{2,1,0:T(8,128)S(1)}, f32[18,16,128]{2,1,0:T(8,128)S(1)}, u32[]{:S(2)}, u32[]{:S(2)}) collective-permute-start(f32[18,16,128]{2,1,0:T(8,128)S(1)} %bitcast.35), channel_id=1, source_target_pairs={{0,16},{16,0},{1,17},{17,1},{2,18},{18,2},{3,19},{19,3},{4,20},{20... | collective-permute-start | bytes 442376 | tf_op jit(solution)/shard_map/ppermute | solution.py:525
  8.6 0.0 collective-permute-start
  8.6 0.2 collective-permute-start.1
  8.7 8.2 %all-to-all-start = ((f32[16,1,128]{2,1,0:T(1,128)}), f32[16,1,128]{2,1,0:T(1,128)S(1)}, u32[]{:S(2)}, u32[]{:S(2)}) async-start(f32[16,1,128]{2,1,0:T(1,128)} %bitcast.12), calls=%async_computation | async-start | bytes 16384 | tf_op jit(solution)/shard_map/all_to_all | solution.py:528
  18.2 0.9 %all-to-all-done = f32[16,1,128]{2,1,0:T(1,128)S(1)} async-done(((f32[16,1,128]{2,1,0:T(1,128)}), f32[16,1,128]{2,1,0:T(1,128)S(1)}, u32[]{:S(2)}, u32[]{:S(2)}) %all-to-all-start) | async-done | bytes 8224 | tf_op jit(solution)/shard_map/all_to_all | solution.py:528
  19.1 0.0 collective-permute-done.edge_ya
  19.1 0.0 collective-permute-done.1.edge_yb
  19.1 0.0 collective-permute-done.2.rest_0_
  19.1 0.0 copy-done.10
  19.1 0.0 copy-done.9
  19.1 0.0 copy-done.8
  19.1 0.0 copy-done.7
  19.1 0.0 copy-done.6
  19.2 0.0 copy-done.5
  19.2 0.0 copy-done.3
  19.2 0.0 copy-done.2
  19.2 0.0 copy-done.1
  19.2 0.0 copy-done.11
  19.2 0.0 copy-done
  19.2 0.0 copy-done.4
  19.2 2.2 %flux.1 = (f32[16,128,128]{2,1,0:T(8,128)}, f32[1,32]{1,0:T(1,128)}) custom-call(f32[16,144,128]{2,1,0:T(8,128)S(1)} %get-tuple-element.14.carried, f32[128,128]{1,0:T(8,128)S(1)} %bitcast.20, f32[128,128]{1,0:T(8,128)S(1)} %bitcast.24, f32[128,128]{1,0:T(8,128)S(1)} %bitcast.25, s32[128,128]{1,0:T(8,128)S(1)} %bitcast.22, f32[16,128,128]{2,1,0:T(8,128)S(1)} %bitcast.18, ...), custom_call_target="tpu_custom_call" | custom-call | tf_op jit(solution)/shard_map/flux/pallas_call | solution.py:532
Async XLA Ops:
  0.6 18.5 %copy-start.10 = (f32[1,32]{1,0:T(1,128)S(1)}, f32[1,32]{1,0:T(1,128)}, u32[]{:S(2)}) copy-start(f32[1,32]{1,0:T(1,128)} %own_press.1) | copy-start | bytes 388
  0.6 18.5 %copy-start.9 = (s32[1,16]{1,0:T(1,128)S(1)}, s32[1,16]{1,0:T(1,128)}, u32[]{:S(2)}) copy-start(s32[1,16]{1,0:T(1,128)} %place.1) | copy-start | bytes 196
  0.7 18.5 %copy-start.8 = (f32[256]{0:T(256)S(1)}, f32[256]{0:T(256)}, u32[]{:S(2)}) copy-start(f32[256]{0:T(256)} %param.42) | copy-start | bytes 3076
  0.7 18.5 %copy-start.7 = (s32[256]{0:T(256)S(1)}, s32[256]{0:T(256)}, u32[]{:S(2)}) copy-start(s32[256]{0:T(256)} %param.41) | copy-start | bytes 3076
  0.7 18.5 %copy-start.6 = (s32[256,1]{0,1:T(1,128)S(1)}, s32[256,1]{0,1:T(1,128)}, u32[]{:S(2)}) copy-start(s32[256,1]{0,1:T(1,128)} %param.40) | copy-start | bytes 3076
  0.7 18.5 %copy-start.5 = (s32[256]{0:T(256)S(1)}, s32[256]{0:T(256)}, u32[]{:S(2)}) copy-start(s32[256]{0:T(256)} %param.39) | copy-start | bytes 3076
  0.7 18.5 %copy-start.3 = (f32[8,16,128]{2,1,0:T(8,128)S(1)}, f32[8,16,128]{2,1,0:T(8,128)}, u32[]{:S(2)}) copy-start(f32[8,16,128]{2,1,0:T(8,128)} %param.28) | copy-start | bytes 196612
  0.7 18.5 %copy-start.2 = (s32[8,16,128]{2,1,0:T(8,128)S(1)}, s32[8,16,128]{2,1,0:T(8,128)}, u32[]{:S(2)}) copy-start(s32[8,16,128]{2,1,0:T(8,128)} %param.27) | copy-start | bytes 196612
  0.7 18.5 %copy-start.1 = (f32[8,16,128]{2,1,0:T(8,128)S(1)}, f32[8,16,128]{2,1,0:T(8,128)}, u32[]{:S(2)}) copy-start(f32[8,16,128]{2,1,0:T(8,128)} %param.25) | copy-start | bytes 196612
  0.7 18.5 %copy-start.11 = (s32[1,32]{1,0:T(1,128)S(1)}, s32[1,32]{1,0:T(1,128)}, u32[]{:S(2)}) copy-start(s32[1,32]{1,0:T(1,128)} %order.1) | copy-start | bytes 388
  0.7 18.5 %copy-start = (f32[16,8,16,128]{3,2,1,0:T(8,128)S(1)}, f32[16,8,16,128]{3,2,1,0:T(8,128)}, u32[]{:S(2)}) copy-start(f32[16,8,16,128]{3,2,1,0:T(8,128)} %param.30) | copy-start | bytes 3145732
  0.7 18.5 %copy-start.4 = (f32[8,16,128]{2,1,0:T(8,128)S(1)}, f32[8,16,128]{2,1,0:T(8,128)}, u32[]{:S(2)}) copy-start(f32[8,16,128]{2,1,0:T(8,128)} %param.29) | copy-start | bytes 196612
  5.6 13.5 %collective-permute-start.2 = (f32[18,16,128]{2,1,0:T(8,128)S(1)}, f32[18,16,128]{2,1,0:T(8,128)S(1)}, u32[]{:S(2)}, u32[]{:S(2)}) collective-permute-start(f32[18,16,128]{2,1,0:T(8,128)S(1)} %bitcast.35), channel_id=1, source_target_pairs={{0,16},{16,0},{1,17},{17,1},{2,18},{18,2},{3,19},{19,3},{4,20},{20... | collective-permute-start | bytes 442376 | tf_op jit(solution)/shard_map/ppermute | solution.py:525
  8.6 10.5 %collective-permute-start = (f32[18,8,128]{2,1,0:T(8,128)S(1)}, f32[18,8,128]{2,1,0:T(8,128)S(1)}, u32[]{:S(2)}, u32[]{:S(2)}) collective-permute-start(f32[18,8,128]{2,1,0:T(8,128)S(1)} %get-tuple-element.16), channel_id=1, source_target_pairs={{0,1},{2,3},{4,5},{6,7},{8,9},{10,11},{12,13},{14,15},{1,0},{3,2},... | collective-permute-start | bytes 221192 | tf_op jit(solution)/shard_map/ppermute | solution.py:524
  8.6 10.5 %collective-permute-start.1 = (f32[18,8,128]{2,1,0:T(8,128)S(1)}, f32[18,8,128]{2,1,0:T(8,128)S(1)}, u32[]{:S(2)}, u32[]{:S(2)}) collective-permute-start(f32[18,8,128]{2,1,0:T(8,128)S(1)} %get-tuple-element.17), channel_id=1, source_target_pairs={{0,16},{1,2},{2,1},{3,4},{4,3},{5,6},{6,5},{7,8},{8,7},{9,10},{10,... | collective-permute-start | bytes 221192 | tf_op jit(solution)/shard_map/ppermute | solution.py:526
  8.7 10.4 %all-to-all-start = ((f32[16,1,128]{2,1,0:T(1,128)}), f32[16,1,128]{2,1,0:T(1,128)S(1)}, u32[]{:S(2)}, u32[]{:S(2)}) async-start(f32[16,1,128]{2,1,0:T(1,128)} %bitcast.12), calls=%async_computation | async-start | bytes 16384 | tf_op jit(solution)/shard_map/all_to_all | solution.py:528
